TPU v7x, 32 devices: a whole 2x2x4 slice. The times are simulated.
32 devices in a mesh: section: 4 (over y, core), dp: 8 (over z, x).
Axes of the slice: x: 2, y: 2, z: 4, core: 2. Of those that a mesh axis runs over, the one named last changes fastest.
Arguments:
- block_input: bfloat16 [6144, 768], P('dp', 'section'), may hold values from -6 to 6
- cotangent: bfloat16 [6144, 768], P('dp', 'section'), may hold values from -6 to 6
- grid_sizes: int32 [16, 2, 2], P('dp'), may hold values from 8 to 13
- section_weight: bfloat16 [4, 768, 4608], P('section'), may hold values from -4 to 4
- norm_gain: float32 [4, 768], P('section'), may hold values from 0.5 to 1.5
- norm_bias: float32 [4, 768], P('section'), may hold values from -1 to 1
- first_vector: float32 [4, 3072], P('section'), may hold values from -2 to 2
- second_vector: float32 [4, 768], P('section'), may hold values from -1.5 to 1.5
Outputs:
- activations: bfloat16 [4, 6144, 768], P('section', 'dp')
- input_grads: bfloat16 [4, 6144, 768], P('section', 'dp')
- section_weight_grad: float32 [4, 768, 4608], P('section')
- norm_gain_grad: float32 [4, 768], P('section')
- norm_bias_grad: float32 [4, 768], P('section')
- first_vector_grad: float32 [4, 3072], P('section')
- second_vector_grad: float32 [4, 768], P('section')
Inputs may be any that keep to these rules, and one draw needn't show every extreme that they name: `grid_sizes`: each packed row holds two images laid out from slot 0; the rest of the row is padding.
All inputs are finite; a program needn't handle non-finite values.
Results may differ from a plain program's by a relative error of at most 0.015.
Values may be sent and summed in bfloat16 or wider, within the bound.
No kernel may reach another device: no remote copies, remote signals or barrier semaphores. Data moves between devices by JAX's collectives and lax.ppermute only.
A program may use at most 192 MiB of HBM per device.

v0:
```python
import jax
import jax.numpy as jnp
from jax import lax
from jax.sharding import PartitionSpec as P

D = 768
HEADS = 12
HEAD_DIM = 64
FF = 3072
ROW_LEN = 384


def shifted(array, axis, by):
    devices = lax.axis_size(axis)
    pairs = [(i, i + by) for i in range(devices) if 0 <= i + by < devices]
    return lax.ppermute(array, axis, pairs)


def for_sending(array):
    return jax.tree.map(lambda a: a.astype(jnp.bfloat16) if a.dtype == jnp.float32 else a, array)


def layout(grid_rows, row_len):
    heights = grid_rows[:, :, 0]
    widths = grid_rows[:, :, 1]
    counts = heights * widths
    end_one = counts[:, 0:1]
    end_two = end_one + counts[:, 1:2]
    places = jnp.arange(row_len, dtype=jnp.int32)[None, :]
    segment = (places >= end_one).astype(jnp.int32) + (places >= end_two).astype(jnp.int32)
    offset = jnp.where(segment == 0, 0, end_one)
    across = jnp.where(segment == 0, widths[:, 0:1], widths[:, 1:2])
    inside = places - offset
    row_pos = jnp.where(segment < 2, inside // across, 0).astype(jnp.float32)
    col_pos = jnp.where(segment < 2, inside % across, 0).astype(jnp.float32)
    return (segment, row_pos, col_pos)


def normalize_parts(field_in, gain_vec, shift_vec):
    center = field_in - jnp.mean(field_in, axis=-1, keepdims=True)
    inverse = lax.rsqrt(jnp.mean(center * center, axis=-1, keepdims=True) + 1e-06)
    scaled = center * inverse
    return (scaled * gain_vec + shift_vec, scaled, inverse)


def norm_back(grad_norm, scaled, inverse, gain_vec):
    grad_scaled = grad_norm * gain_vec
    grad_field = inverse * (
        grad_scaled
        - jnp.mean(grad_scaled, axis=-1, keepdims=True)
        - scaled * jnp.mean(grad_scaled * scaled, axis=-1, keepdims=True)
    )
    return (grad_field, jnp.sum(grad_norm * scaled, axis=0), jnp.sum(grad_norm, axis=0))


def rotate(values, cosine, sine_part):
    halfway = values.shape[-1] // 2
    leading = values[..., :halfway]
    trailing = values[..., halfway:]
    return jnp.concatenate(
        [leading * cosine - trailing * sine_part, trailing * cosine + leading * sine_part], axis=-1
    )


def unrotate(grad_rot, rotated, cosine, sine_part):
    halfway = grad_rot.shape[-1] // 2
    grad_lead = grad_rot[..., :halfway]
    grad_trail = grad_rot[..., halfway:]
    grad_pre = jnp.concatenate(
        [grad_lead * cosine + grad_trail * sine_part, grad_trail * cosine - grad_lead * sine_part],
        axis=-1,
    )
    grad_angle = grad_trail * rotated[..., :halfway] - grad_lead * rotated[..., halfway:]
    return (grad_pre, grad_angle)


def attention_parts(
    field_in, weights, first_vec, second_vec, gain_vec, shift_vec, segment, row_pos, col_pos
):
    length = field_in.shape[0]
    score_scale = HEAD_DIM ** (-0.5)
    wide_in = field_in.astype(jnp.float32)
    normed, scaled, inverse = normalize_parts(wide_in, gain_vec, shift_vec)
    normed_low = normed.astype(jnp.bfloat16)
    packed = (
        jnp.dot(normed_low, weights[:, : 3 * D], preferred_element_type=jnp.float32)
        + first_vec[: 3 * D]
    )
    freq_x = first_vec[3 * D : 3 * D + D // 2].reshape(HEADS, HEAD_DIM // 2)
    freq_y = first_vec[3 * D + D // 2 :].reshape(HEADS, HEAD_DIM // 2)
    angles = col_pos[:, None, None] * freq_x[None] + row_pos[:, None, None] * freq_y[None]
    cosine = jnp.cos(angles)
    sine_part = jnp.sin(angles)
    query_rot = rotate(packed[:, :D].reshape(length, HEADS, HEAD_DIM), cosine, sine_part)
    key_rot = rotate(packed[:, D : 2 * D].reshape(length, HEADS, HEAD_DIM), cosine, sine_part)
    query_low = query_rot.astype(jnp.bfloat16)
    key_low = key_rot.astype(jnp.bfloat16)
    value_low = packed[:, 2 * D :].reshape(length, HEADS, HEAD_DIM).astype(jnp.bfloat16)
    scores = (
        jnp.einsum("qhd,khd->hqk", query_low, key_low, preferred_element_type=jnp.float32)
        * score_scale
    )
    same_image = (segment[:, None] == segment[None, :])[None]
    scores = jnp.where(same_image, scores, -1e30)
    exponent = jnp.exp(scores - jnp.max(scores, axis=-1, keepdims=True))
    attn_probs = exponent / jnp.sum(exponent, axis=-1, keepdims=True)
    probs_low = attn_probs.astype(jnp.bfloat16)
    mixed_out = jnp.einsum("hqk,khd->qhd", probs_low, value_low, preferred_element_type=jnp.float32)
    mixed_low = mixed_out.reshape(length, D).astype(jnp.bfloat16)
    branch = (
        jnp.dot(mixed_low, weights[:, 3 * D : 4 * D], preferred_element_type=jnp.float32)
        + second_vec
    )
    return (
        wide_in,
        normed_low,
        scaled,
        inverse,
        cosine,
        sine_part,
        query_rot,
        key_rot,
        query_low,
        key_low,
        value_low,
        attn_probs,
        probs_low,
        mixed_low,
        branch,
    )


def attention_back(
    field_in,
    grad_out,
    weights,
    first_vec,
    second_vec,
    gain_vec,
    shift_vec,
    segment,
    row_pos,
    col_pos,
):
    parts = attention_parts(
        field_in, weights, first_vec, second_vec, gain_vec, shift_vec, segment, row_pos, col_pos
    )
    (
        wide_in,
        normed_low,
        scaled,
        inverse,
        cosine,
        sine_part,
        query_rot,
        key_rot,
        query_low,
        key_low,
        value_low,
        attn_probs,
        probs_low,
        mixed_low,
        branch,
    ) = parts
    length = field_in.shape[0]
    score_scale = HEAD_DIM ** (-0.5)
    grad_wide = grad_out.astype(jnp.float32)
    grad_second = jnp.sum(grad_wide, axis=0)
    grad_w_out = jnp.einsum("td,te->de", mixed_low, grad_out, preferred_element_type=jnp.float32)
    grad_mixed = jnp.einsum(
        "te,de->td", grad_out, weights[:, 3 * D : 4 * D], preferred_element_type=jnp.float32
    )
    grad_mixed = grad_mixed.astype(jnp.bfloat16).reshape(length, HEADS, HEAD_DIM)
    grad_probs = jnp.einsum(
        "qhd,khd->hqk", grad_mixed, value_low, preferred_element_type=jnp.float32
    )
    grad_value = jnp.einsum(
        "hqk,qhd->khd", probs_low, grad_mixed, preferred_element_type=jnp.float32
    )
    grad_scores = attn_probs * (
        grad_probs - jnp.sum(grad_probs * attn_probs, axis=-1, keepdims=True)
    )
    grad_scores_low = grad_scores.astype(jnp.bfloat16)
    grad_query = (
        jnp.einsum("hqk,khd->qhd", grad_scores_low, key_low, preferred_element_type=jnp.float32)
        * score_scale
    )
    grad_key = (
        jnp.einsum("hqk,qhd->khd", grad_scores_low, query_low, preferred_element_type=jnp.float32)
        * score_scale
    )
    grad_query_pre, angle_query = unrotate(grad_query, query_rot, cosine, sine_part)
    grad_key_pre, angle_key = unrotate(grad_key, key_rot, cosine, sine_part)
    grad_angle = angle_query + angle_key
    grad_freq_x = jnp.einsum("thj,t->hj", grad_angle, col_pos).reshape(-1)
    grad_freq_y = jnp.einsum("thj,t->hj", grad_angle, row_pos).reshape(-1)
    grad_packed = jnp.concatenate(
        [
            grad_query_pre.reshape(length, D),
            grad_key_pre.reshape(length, D),
            grad_value.reshape(length, D),
        ],
        axis=1,
    ).astype(jnp.bfloat16)
    grad_w_in = jnp.einsum("td,te->de", normed_low, grad_packed, preferred_element_type=jnp.float32)
    grad_bias_in = jnp.sum(grad_packed.astype(jnp.float32), axis=0)
    grad_normed = jnp.einsum(
        "te,de->td", grad_packed, weights[:, : 3 * D], preferred_element_type=jnp.float32
    )
    grad_field, grad_gain, grad_shift = norm_back(grad_normed, scaled, inverse, gain_vec)
    grad_in = (grad_wide + grad_field).astype(jnp.bfloat16)
    lead_delta = jnp.concatenate([grad_w_in, grad_w_out], axis=1)
    trail_delta = jnp.zeros((D, FF), jnp.float32)
    grad_first = jnp.concatenate([grad_bias_in, grad_freq_x, grad_freq_y])
    return (grad_in, lead_delta, trail_delta, grad_gain, grad_shift, grad_first, grad_second)


def feed_parts(field_in, weights, borrowed, first_vec, second_vec, gain_vec, shift_vec):
    wide_in = field_in.astype(jnp.float32)
    normed, scaled, inverse = normalize_parts(wide_in, gain_vec, shift_vec)
    normed_low = normed.astype(jnp.bfloat16)
    hidden = jnp.dot(normed_low, weights[:, :FF], preferred_element_type=jnp.float32) + first_vec
    active_low = jax.nn.gelu(hidden).astype(jnp.bfloat16)
    down_t = jnp.concatenate([borrowed, weights[:, FF:]], axis=1)
    branch = (
        jnp.einsum("tf,df->td", active_low, down_t, preferred_element_type=jnp.float32) + second_vec
    )
    return (wide_in, normed_low, scaled, inverse, hidden, active_low, down_t, branch)


def feed_back(field_in, grad_out, weights, borrowed, first_vec, second_vec, gain_vec, shift_vec):
    wide_in, normed_low, scaled, inverse, hidden, active_low, down_t, branch = feed_parts(
        field_in, weights, borrowed, first_vec, second_vec, gain_vec, shift_vec
    )
    grad_wide = grad_out.astype(jnp.float32)
    grad_second = jnp.sum(grad_wide, axis=0)
    grad_down = jnp.einsum("td,tf->df", grad_out, active_low, preferred_element_type=jnp.float32)
    grad_active = jnp.dot(grad_out, down_t, preferred_element_type=jnp.float32)
    gelu_pull = jax.vjp(jax.nn.gelu, hidden)[1]
    grad_hidden = gelu_pull(grad_active)[0].astype(jnp.bfloat16)
    grad_w_in = jnp.einsum("td,tf->df", normed_low, grad_hidden, preferred_element_type=jnp.float32)
    grad_first = jnp.sum(grad_hidden.astype(jnp.float32), axis=0)
    grad_normed = jnp.einsum(
        "tf,df->td", grad_hidden, weights[:, :FF], preferred_element_type=jnp.float32
    )
    grad_field, grad_gain, grad_shift = norm_back(grad_normed, scaled, inverse, gain_vec)
    grad_in = (grad_wide + grad_field).astype(jnp.bfloat16)
    return (grad_in, grad_w_in, grad_down, grad_gain, grad_shift, grad_first, grad_second)


def body(
    block_input,
    cotangent,
    grid_sizes,
    section_weight,
    norm_gain,
    norm_bias,
    first_vector,
    second_vector,
):
    section_no = lax.axis_index("section")
    parity = section_no % 2
    micro_count = grid_sizes.shape[0]
    field_all, cotan_all = (
        lax.all_gather(block_input, "section", axis=1, tiled=True),
        lax.all_gather(cotangent, "section", axis=1, tiled=True),
    )
    field_all = field_all.reshape(micro_count, ROW_LEN, D)
    cotan_all = cotan_all.reshape(micro_count, ROW_LEN, D)
    weights = section_weight[0]
    gain_vec = norm_gain[0]
    shift_vec = norm_bias[0]
    first_vec = first_vector[0]
    second_vec = second_vector[0]
    borrowed = shifted(weights[:, FF:], "section", 1)
    segment, row_pos, col_pos = layout(grid_sizes, ROW_LEN)
    tick_count = micro_count + 3

    def spare_forward(field_in, which):
        return jnp.zeros_like(field_in)

    def attention_forward(field_in, which):
        parts = attention_parts(
            field_in,
            weights,
            first_vec,
            second_vec,
            gain_vec,
            shift_vec,
            segment[which],
            row_pos[which],
            col_pos[which],
        )
        return (parts[0] + parts[-1]).astype(jnp.bfloat16)

    def feed_forward(field_in, which):
        parts = feed_parts(field_in, weights, borrowed, first_vec, second_vec, gain_vec, shift_vec)
        return (parts[0] + parts[-1]).astype(jnp.bfloat16)

    def forward_tick(tick, carry):
        arrived, saved_in, results = carry
        micro_no = tick - section_no
        active = (micro_no >= 0) & (micro_no < micro_count)
        which = jnp.clip(micro_no, 0, micro_count - 1)
        incoming = jnp.where(section_no == 0, field_all[which], arrived)
        choose = jnp.where(active, 1 + parity, 0)
        produced = lax.switch(
            choose, [spare_forward, attention_forward, feed_forward], incoming, which
        )
        saved_in = saved_in.at[which].set(jnp.where(active, incoming, saved_in[which]))
        results = results.at[which].set(jnp.where(active, produced, results[which]))
        arrived = jax.tree.map(
            lambda part, own: part.astype(own.dtype),
            shifted(for_sending(produced), "section", 1),
            produced,
        )
        return (arrived, saved_in, results)

    blank = jnp.zeros((ROW_LEN, D), jnp.bfloat16)
    stacked_blank = jnp.zeros((micro_count, ROW_LEN, D), jnp.bfloat16)
    arrived, saved_in, results = lax.fori_loop(
        0, tick_count, forward_tick, (blank, stacked_blank, stacked_blank)
    )

    def spare_backward(field_in, grad_out, which):
        return (
            jnp.zeros_like(grad_out),
            jnp.zeros((D, FF), jnp.float32),
            jnp.zeros((D, FF), jnp.float32),
            jnp.zeros((D,), jnp.float32),
            jnp.zeros((D,), jnp.float32),
            jnp.zeros((FF,), jnp.float32),
            jnp.zeros((D,), jnp.float32),
        )

    def attention_backward(field_in, grad_out, which):
        return attention_back(
            field_in,
            grad_out,
            weights,
            first_vec,
            second_vec,
            gain_vec,
            shift_vec,
            segment[which],
            row_pos[which],
            col_pos[which],
        )

    def feed_backward(field_in, grad_out, which):
        return feed_back(
            field_in, grad_out, weights, borrowed, first_vec, second_vec, gain_vec, shift_vec
        )

    def backward_tick(tick, carry):
        (
            arrived_grad,
            grad_lead,
            grad_trail,
            grad_gain,
            grad_shift,
            grad_first,
            grad_second,
            grads_in,
        ) = carry
        micro_no = tick - (3 - section_no)
        active = (micro_no >= 0) & (micro_no < micro_count)
        which = jnp.clip(micro_no, 0, micro_count - 1)
        incoming = jnp.where(section_no == 3, cotan_all[which], arrived_grad)
        choose = jnp.where(active, 1 + parity, 0)
        outcome = lax.switch(
            choose,
            [spare_backward, attention_backward, feed_backward],
            saved_in[which],
            incoming,
            which,
        )
        grad_lead = grad_lead + outcome[1]
        grad_trail = grad_trail + outcome[2]
        grad_gain = grad_gain + outcome[3]
        grad_shift = grad_shift + outcome[4]
        grad_first = grad_first + outcome[5]
        grad_second = grad_second + outcome[6]
        grads_in = grads_in.at[which].set(jnp.where(active, outcome[0], grads_in[which]))
        arrived_grad = shifted(for_sending(outcome[0]), "section", -1)
        return (
            arrived_grad,
            grad_lead,
            grad_trail,
            grad_gain,
            grad_shift,
            grad_first,
            grad_second,
            grads_in,
        )

    start_carry = (
        blank,
        jnp.zeros((D, FF), jnp.float32),
        jnp.zeros((D, FF), jnp.float32),
        jnp.zeros((D,), jnp.float32),
        jnp.zeros((D,), jnp.float32),
        jnp.zeros((FF,), jnp.float32),
        jnp.zeros((D,), jnp.float32),
        stacked_blank,
    )
    finished = lax.fori_loop(0, tick_count, backward_tick, start_carry)
    grad_lead, grad_trail, grad_gain, grad_shift, grad_first, grad_second, grads_in = finished[1:]
    summed = lax.psum((grad_lead, grad_trail, grad_gain, grad_shift, grad_first, grad_second), "dp")
    returned = shifted(summed[1][:, : FF // 2].astype(jnp.bfloat16), "section", -1).astype(
        jnp.float32
    )
    own_tail = jnp.where(parity == 0, returned, summed[1][:, FF // 2 :])
    weight_grad = jnp.concatenate([summed[0], own_tail], axis=1)
    gain_total, shift_total, first_total, second_total = (
        summed[2],
        summed[3],
        summed[4],
        summed[5],
    )
    activations = results.reshape(1, micro_count * ROW_LEN, D)
    input_grads = grads_in.reshape(1, micro_count * ROW_LEN, D)
    return (
        activations,
        input_grads,
        weight_grad[None],
        gain_total[None],
        shift_total[None],
        first_total[None],
        second_total[None],
    )


def solution(mesh):
    in_specs = (
        P("dp", "section"),
        P("dp", "section"),
        P("dp", None, None),
        P("section", None, None),
        P("section", None),
        P("section", None),
        P("section", None),
        P("section", None),
    )
    out_specs = (
        P("section", "dp", None),
        P("section", "dp", None),
        P("section", None, None),
        P("section", None),
        P("section", None),
        P("section", None),
        P("section", None),
    )
    return jax.shard_map(body, mesh=mesh, in_specs=in_specs, out_specs=out_specs, check_vma=False)
```

profile of v0, /device:TPU:0, one launch (start us, length us, event | category | flops | bytes accessed | tf_op | source)
XLA Modules:
  0.0 1330.3 jit_solution(16659861977057137823)
XLA Ops:
  14.7 15.1 %all-gather.3.cloned.1.call-done = bf16[768,768]{0,1:T(8,128)(2,1)} async-done(((bf16[768,192]{0,1:T(8,128)(2,1)}), bf16[768,768]{0,1:T(8,128)(2,1)}) %all-gather.3.cloned.1.call-update) | async-done | bytes 1179664 | tf_op jit(solution)/shard_map/all_gather | solution.py:265
  32.1 19.9 %all-gather.5.cloned.1.call-done = bf16[768,768]{0,1:T(8,128)(2,1)} async-done(((bf16[768,192]{0,1:T(8,128)(2,1)}), bf16[768,768]{0,1:T(8,128)(2,1)}) %all-gather.5.cloned.1.call-update) | async-done | bytes 1179664 | tf_op jit(solution)/shard_map/all_gather | solution.py:266
  55.6 169.8 %while.56 = (s32[]{:T(128)}, bf16[384,768]{1,0:T(8,128)(2,1)S(1)}, bf16[2,384,768]{2,1,0:T(8,128)(2,1)S(1)}, bf16[2,384,768]{2,1,0:T(8,128)(2,1)}, s32[]{:T(128)...) while((s32[]{:T(128)}, bf16[384,768]{1,0:T(8,128)(2,1)S(1)}, ...), condition=%wide.region_11.12_spmd.clone.clone, body=%wide.region_0.11_spmd.clone.clone.sunk | while | flops 3651331328 | bytes 77210376 | solution.py:321
  61.7 29.2 %conditional.9 = (bf16[384,768]{1,0:T(8,128)(2,1)S(1)}) conditional(s32[]{:T(128)} %clamp.25, () %tuple.204, (bf16[384,768]{1,0:T(8,128)(2,1)S(1)}, f32[1,768]{1,0:T(1,128)S(1)}, f32[1,768]{1,0:T(1,128)S(1)}, bf16[768,4608]{1,0:T(8,128)(2,1)}, f32[3072]{0:T(1024)S(1)}, /*index=5*/s32[]{:T(128)}, s32[2,384]{1,0:T(2,128)}, ...), branch_computations={%region_1.1_spmd, %region_2.6_spmd, %region_7.9_spmd} | conditional | flops 3649831424 | bytes 58275984 | solution.py:307
  77.3 6.3 fusion.206
  101.2 29.2 %conditional.9 = (bf16[384,768]{1,0:T(8,128)(2,1)S(1)}) conditional(s32[]{:T(128)} %clamp.25, () %tuple.204, (bf16[384,768]{1,0:T(8,128)(2,1)S(1)}, f32[1,768]{1,0:T(1,128)S(1)}, f32[1,768]{1,0:T(1,128)S(1)}, bf16[768,4608]{1,0:T(8,128)(2,1)}, f32[3072]{0:T(1024)S(1)}, /*index=5*/s32[]{:T(128)}, s32[2,384]{1,0:T(2,128)}, ...), branch_computations={%region_1.1_spmd, %region_2.6_spmd, %region_7.9_spmd} | conditional | flops 3649831424 | bytes 58275984 | solution.py:307
  116.8 6.3 fusion.206
  140.7 13.4 %collective-permute-start = (bf16[384,768]{1,0:T(8,128)(2,1)S(1)}, bf16[384,768]{1,0:T(8,128)(2,1)S(1)}, u32[]{:S(2)}, u32[]{:S(2)}) collective-permute-start(bf16[384,768]{1,0:T(8,128)(2,1)S(1)} %get-tuple-element.2103), channel_id=1, source_target_pairs={{0,8},{8,16},{16,24},{1,9},{9,17},{17,25},{2,10},{10,18},{18,26},{... | collective-permute-start | bytes 1769480 | tf_op jit(solution)/shard_map/while/body/eval_jaxpr/ppermute | solution.py:16
  162.9 13.1 collective-permute-start
  184.9 37.7 %collective-permute-start = (bf16[384,768]{1,0:T(8,128)(2,1)S(1)}, bf16[384,768]{1,0:T(8,128)(2,1)S(1)}, u32[]{:S(2)}, u32[]{:S(2)}) collective-permute-start(bf16[384,768]{1,0:T(8,128)(2,1)S(1)} %get-tuple-element.2103), channel_id=1, source_target_pairs={{0,8},{8,16},{16,24},{1,9},{9,17},{17,25},{2,10},{10,18},{18,26},{... | collective-permute-start | bytes 1769480 | tf_op jit(solution)/shard_map/while/body/eval_jaxpr/ppermute | solution.py:16
  226.6 477.2 %while.57 = (s32[]{:T(128)}, bf16[384,768]{1,0:T(8,128)(2,1)S(1)}, f32[768,3072]{1,0:T(8,128)}, f32[768,3072]{1,0:T(8,128)}, f32[768]{0:T(1024)}, /*index=5*/f32...) while((s32[]{:T(128)}, bf16[384,768]{1,0:T(8,128)(2,1)S(1)}, ...), condition=%wide.region_36.37_spmd.clone.clone.clone, body=%wide.region_12.36_spmd.clone.clone.clone.sunk | while | flops 9129032704 | bytes 302151360 | solution.py:407
  253.5 13.0 conditional.10
  271.4 16.5 %select_add_fusion.10 = (f32[768,3072]{1,0:T(8,128)}, f32[768,3072]{1,0:T(8,128)}) fusion(f32[768,3072]{1,0:T(8,128)} %get-tuple-element.1911, f32[768,3072]{1,0:T(8,128)} %get-tuple-element.2046, pred[]{:T(512)S(6)} %compare.79, f32[768,3072]{1,0:T(8,128)} %get-tuple-element.1912, f32[768,3072]{1,0:T(8,128)} %get-tuple-element.2045), kind=kLoop, calls=%fused_computation.269.clone.1 | loop fusion | flops 9437184 | bytes 56623104 | tf_op jit(solution)/shard_map/while/body/eval_jaxpr/add | solution.py:379
  295.1 13.0 conditional.10
  313.1 21.3 %select_add_fusion.10 = (f32[768,3072]{1,0:T(8,128)}, f32[768,3072]{1,0:T(8,128)}) fusion(f32[768,3072]{1,0:T(8,128)} %get-tuple-element.1911, f32[768,3072]{1,0:T(8,128)} %get-tuple-element.2046, pred[]{:T(512)S(6)} %compare.79, f32[768,3072]{1,0:T(8,128)} %get-tuple-element.1912, f32[768,3072]{1,0:T(8,128)} %get-tuple-element.2045), kind=kLoop, calls=%fused_computation.269.clone.1 | loop fusion | flops 9437184 | bytes 56623104 | tf_op jit(solution)/shard_map/while/body/eval_jaxpr/add | solution.py:379
  341.6 13.0 conditional.10
  359.6 21.3 %select_add_fusion.10 = (f32[768,3072]{1,0:T(8,128)}, f32[768,3072]{1,0:T(8,128)}) fusion(f32[768,3072]{1,0:T(8,128)} %get-tuple-element.1911, f32[768,3072]{1,0:T(8,128)} %get-tuple-element.2046, pred[]{:T(512)S(6)} %compare.79, f32[768,3072]{1,0:T(8,128)} %get-tuple-element.1912, f32[768,3072]{1,0:T(8,128)} %get-tuple-element.2045), kind=kLoop, calls=%fused_computation.269.clone.1 | loop fusion | flops 9437184 | bytes 56623104 | tf_op jit(solution)/shard_map/while/body/eval_jaxpr/add | solution.py:379
  383.8 72.8 %collective-permute-done.1 = bf16[384,768]{1,0:T(8,128)(2,1)S(1)} collective-permute-done((bf16[384,768]{1,0:T(8,128)(2,1)}, bf16[384,768]{1,0:T(8,128)(2,1)S(1)}, u32[]{:S(2)}, u32[]{:S(2)}) %collective-permute-start.1) | collective-permute-done | bytes 589856 | tf_op jit(solution)/shard_map/while/body/eval_jaxpr/ppermute | solution.py:16
  459.8 87.7 %conditional.10 = (bf16[384,768]{1,0:T(8,128)(2,1)}, f32[768,3072]{1,0:T(8,128)}, f32[768,3072]{1,0:T(8,128)}, f32[768]{0:T(1024)}, f32[768]{0:T(1024)}, /*index=5*/f32[3072]{0:T(1024)}, f32[768]{0:T(1024)}) conditional(s32[]{:T(128)} %clamp.26, () %tuple.211, (bf16[384,768]{1,0:T(8,128)(2,1)S(1)}, ...), branch_computations={%region_13.13_spmd, %region_14.25_spmd, %region_26.34_spmd} | conditional | flops 9118673920 | bytes 218125088 | solution.py:371
  480.0 7.1 fusion.209
  496.3 7.4 multiply_reduce_fusion
  503.7 6.3 multiply_convert_fusion
  527.8 8.1 pad_maximum_fusion.12
  552.5 21.3 %select_add_fusion.10 = (f32[768,3072]{1,0:T(8,128)}, f32[768,3072]{1,0:T(8,128)}) fusion(f32[768,3072]{1,0:T(8,128)} %get-tuple-element.1911, f32[768,3072]{1,0:T(8,128)} %get-tuple-element.2046, pred[]{:T(512)S(6)} %compare.79, f32[768,3072]{1,0:T(8,128)} %get-tuple-element.1912, f32[768,3072]{1,0:T(8,128)} %get-tuple-element.2045), kind=kLoop, calls=%fused_computation.269.clone.1 | loop fusion | flops 9437184 | bytes 56623104 | tf_op jit(solution)/shard_map/while/body/eval_jaxpr/add | solution.py:379
  582.7 87.7 %conditional.10 = (bf16[384,768]{1,0:T(8,128)(2,1)}, f32[768,3072]{1,0:T(8,128)}, f32[768,3072]{1,0:T(8,128)}, f32[768]{0:T(1024)}, f32[768]{0:T(1024)}, /*index=5*/f32[3072]{0:T(1024)}, f32[768]{0:T(1024)}) conditional(s32[]{:T(128)} %clamp.26, () %tuple.211, (bf16[384,768]{1,0:T(8,128)(2,1)S(1)}, ...), branch_computations={%region_13.13_spmd, %region_14.25_spmd, %region_26.34_spmd} | conditional | flops 9118673920 | bytes 218125088 | solution.py:371
  602.9 7.1 fusion.209
  619.2 7.4 multiply_reduce_fusion
  626.6 6.3 multiply_convert_fusion
  650.6 8.1 pad_maximum_fusion.12
  675.3 21.3 %select_add_fusion.10 = (f32[768,3072]{1,0:T(8,128)}, f32[768,3072]{1,0:T(8,128)}) fusion(f32[768,3072]{1,0:T(8,128)} %get-tuple-element.1911, f32[768,3072]{1,0:T(8,128)} %get-tuple-element.2046, pred[]{:T(512)S(6)} %compare.79, f32[768,3072]{1,0:T(8,128)} %get-tuple-element.1912, f32[768,3072]{1,0:T(8,128)} %get-tuple-element.2045), kind=kLoop, calls=%fused_computation.269.clone.1 | loop fusion | flops 9437184 | bytes 56623104 | tf_op jit(solution)/shard_map/while/body/eval_jaxpr/add | solution.py:379
  703.8 568.8 %all-reduce.4.cloned.1.call-done = (f32[768,3072]{1,0:T(8,128)}, f32[768,3072]{1,0:T(8,128)}) async-done(((f32[768,3072]{1,0:T(8,128)}, f32[768,3072]{1,0:T(8,128)}), (f32[768,3072]{1,0:T(8,128)}, f32[768,3072]{1,0:T(8,128)})) %all-reduce.4.cloned.1.call-update) | async-done | bytes 18874384 | tf_op jit(solution)/shard_map/psum | solution.py:409
  1276.7 35.7 %all-reduce = (f32[1,768]{1,0:T(1,128)}, f32[1,768]{1,0:T(1,128)}, f32[1,3072]{1,0:T(1,128)}, f32[1,768]{1,0:T(1,128)}) all-reduce(f32[1,768]{1,0:T(1,128)S(1)} %broadcast_in_dim.106, f32[1,768]{1,0:T(1,128)S(1)} %broadcast_in_dim.107, f32[1,3072]{1,0:T(1,128)S(1)} %bitcast.161, ...), channel_id=1, replica_groups=mesh['section'=4,'dp'=8] {'dp'}, use_global_device_ids=true, to_apply=%region_39.40 | all-reduce | flops 5376 | bytes 43008 | tf_op jit(solution)/shard_map/psum | solution.py:409
  (537 shorter events, 339.9 us)
Async XLA Ops:
  7.2 22.6 %all-gather.3.cloned.1.call-start = ((), (), s32[]{:S(2)}) async-start(), calls=%async_computation | async-start | bytes 1474560 | tf_op jit(solution)/shard_map/all_gather | solution.py:265
  7.9 44.1 %all-gather.5.cloned.1.call-start = ((), (), s32[]{:S(2)}) async-start(), calls=%async_computation.1 | async-start | bytes 1474560 | tf_op jit(solution)/shard_map/all_gather | solution.py:266
  9.8 44.6 %collective-permute-start.2 = (bf16[768,1536]{1,0:T(8,128)(2,1)S(1)}, bf16[768,1536]{1,0:T(8,128)(2,1)}, u32[]{:S(2)}, u32[]{:S(2)}) collective-permute-start(bf16[768,1536]{1,0:T(8,128)(2,1)S(1)} %slice.292), channel_id=1, source_target_pairs={{0,8},{8,16},{16,24},{1,9},{9,17},{17,25},{2,10},{10,18},{18,26},{... | collective-permute-start | bytes 7077896 | tf_op jit(solution)/shard_map/ppermute | solution.py:16
  13.5 1259.1 %all-reduce.4.cloned.1.call-start = ((), (), s32[]{:S(2)}) async-start(), calls=%async_computation.2 | async-start | bytes 37748736 | tf_op jit(solution)/shard_map/psum | solution.py:409
  32.1 23.5 %copy-start.22 = (f32[1,768]{1,0:T(1,128)S(1)}, f32[1,768]{1,0:T(1,128)}, u32[]{:S(2)}) copy-start(f32[1,768]{1,0:T(1,128)} %param.28) | copy-start | bytes 9220
  32.1 23.5 %copy-start.25 = (f32[1,768]{1,0:T(1,128)S(1)}, f32[1,768]{1,0:T(1,128)}, u32[]{:S(2)}) copy-start(f32[1,768]{1,0:T(1,128)} %param.29) | copy-start | bytes 9220
  90.9 4.3 collective-permute-start
  130.4 4.3 collective-permute-start
  140.7 16.2 %collective-permute-start = (bf16[384,768]{1,0:T(8,128)(2,1)S(1)}, bf16[384,768]{1,0:T(8,128)(2,1)S(1)}, u32[]{:S(2)}, u32[]{:S(2)}) collective-permute-start(bf16[384,768]{1,0:T(8,128)(2,1)S(1)} %get-tuple-element.2103), channel_id=1, source_target_pairs={{0,8},{8,16},{16,24},{1,9},{9,17},{17,25},{2,10},{10,18},{18,26},{... | collective-permute-start | bytes 1769480 | tf_op jit(solution)/shard_map/while/body/eval_jaxpr/ppermute | solution.py:16
  162.9 15.9 %collective-permute-start = (bf16[384,768]{1,0:T(8,128)(2,1)S(1)}, bf16[384,768]{1,0:T(8,128)(2,1)S(1)}, u32[]{:S(2)}, u32[]{:S(2)}) collective-permute-start(bf16[384,768]{1,0:T(8,128)(2,1)S(1)} %get-tuple-element.2103), channel_id=1, source_target_pairs={{0,8},{8,16},{16,24},{1,9},{9,17},{17,25},{2,10},{10,18},{18,26},{... | collective-permute-start | bytes 1769480 | tf_op jit(solution)/shard_map/while/body/eval_jaxpr/ppermute | solution.py:16
  184.9 40.5 %copy-start.8 = (bf16[2,384,768]{2,1,0:T(8,128)(2,1)S(1)}, bf16[2,384,768]{2,1,0:T(8,128)(2,1)}, u32[]{:S(2)}) copy-start(bf16[2,384,768]{2,1,0:T(8,128)(2,1)} %copy-done.7) | copy-start | bytes 3538948 | tf_op jit(solution)/shard_map/while
  184.9 40.5 %collective-permute-start = (bf16[384,768]{1,0:T(8,128)(2,1)S(1)}, bf16[384,768]{1,0:T(8,128)(2,1)S(1)}, u32[]{:S(2)}, u32[]{:S(2)}) collective-permute-start(bf16[384,768]{1,0:T(8,128)(2,1)S(1)} %get-tuple-element.2103), channel_id=1, source_target_pairs={{0,8},{8,16},{16,24},{1,9},{9,17},{17,25},{2,10},{10,18},{18,26},{... | collective-permute-start | bytes 1769480 | tf_op jit(solution)/shard_map/while/body/eval_jaxpr/ppermute | solution.py:16
  266.4 24.5 %collective-permute-start.1 = (bf16[384,768]{1,0:T(8,128)(2,1)}, bf16[384,768]{1,0:T(8,128)(2,1)S(1)}, u32[]{:S(2)}, u32[]{:S(2)}) collective-permute-start(bf16[384,768]{1,0:T(8,128)(2,1)} %get-tuple-element.1910), channel_id=1, source_target_pairs={{8,0},{16,8},{24,16},{9,1},{17,9},{25,17},{10,2},{18,10},{26,18},{... | collective-permute-start | bytes 1769480 | tf_op jit(solution)/shard_map/while/body/eval_jaxpr/ppermute | solution.py:16
  308.1 29.2 %collective-permute-start.1 = (bf16[384,768]{1,0:T(8,128)(2,1)}, bf16[384,768]{1,0:T(8,128)(2,1)S(1)}, u32[]{:S(2)}, u32[]{:S(2)}) collective-permute-start(bf16[384,768]{1,0:T(8,128)(2,1)} %get-tuple-element.1910), channel_id=1, source_target_pairs={{8,0},{16,8},{24,16},{9,1},{17,9},{25,17},{10,2},{18,10},{26,18},{... | collective-permute-start | bytes 1769480 | tf_op jit(solution)/shard_map/while/body/eval_jaxpr/ppermute | solution.py:16
  313.1 25.3 %copy-start.10 = (bf16[2,384,768]{2,1,0:T(8,128)(2,1)S(1)}, bf16[2,384,768]{2,1,0:T(8,128)(2,1)}, u32[]{:S(2)}) copy-start(bf16[2,384,768]{2,1,0:T(8,128)(2,1)} %copy-done.9) | copy-start | bytes 3538948 | tf_op jit(solution)/shard_map/while
  313.1 25.3 %copy-start.24 = (f32[1,768]{1,0:T(1,128)S(1)}, f32[1,768]{1,0:T(1,128)}, u32[]{:S(2)}) copy-start(f32[1,768]{1,0:T(1,128)} %copy-done.23) | copy-start | bytes 9220 | tf_op jit(solution)/shard_map/while
  313.1 25.2 %copy-start.27 = (f32[1,768]{1,0:T(1,128)S(1)}, f32[1,768]{1,0:T(1,128)}, u32[]{:S(2)}) copy-start(f32[1,768]{1,0:T(1,128)} %copy-done.26) | copy-start | bytes 9220 | tf_op jit(solution)/shard_map/while
  354.5 102.0 %collective-permute-start.1 = (bf16[384,768]{1,0:T(8,128)(2,1)}, bf16[384,768]{1,0:T(8,128)(2,1)S(1)}, u32[]{:S(2)}, u32[]{:S(2)}) collective-permute-start(bf16[384,768]{1,0:T(8,128)(2,1)} %get-tuple-element.1910), channel_id=1, source_target_pairs={{8,0},{16,8},{24,16},{9,1},{17,9},{25,17},{10,2},{18,10},{26,18},{... | collective-permute-start | bytes 1769480 | tf_op jit(solution)/shard_map/while/body/eval_jaxpr/ppermute | solution.py:16
  359.5 97.0 %copy-start.10 = (bf16[2,384,768]{2,1,0:T(8,128)(2,1)S(1)}, bf16[2,384,768]{2,1,0:T(8,128)(2,1)}, u32[]{:S(2)}) copy-start(bf16[2,384,768]{2,1,0:T(8,128)(2,1)} %copy-done.9) | copy-start | bytes 3538948 | tf_op jit(solution)/shard_map/while
  359.5 97.0 %copy-start.24 = (f32[1,768]{1,0:T(1,128)S(1)}, f32[1,768]{1,0:T(1,128)}, u32[]{:S(2)}) copy-start(f32[1,768]{1,0:T(1,128)} %copy-done.23) | copy-start | bytes 9220 | tf_op jit(solution)/shard_map/while
  359.6 97.0 %copy-start.27 = (f32[1,768]{1,0:T(1,128)S(1)}, f32[1,768]{1,0:T(1,128)}, u32[]{:S(2)}) copy-start(f32[1,768]{1,0:T(1,128)} %copy-done.26) | copy-start | bytes 9220 | tf_op jit(solution)/shard_map/while
  382.9 73.7 %copy-start.33 = (f32[3072]{0:T(1024)}, f32[3072]{0:T(1024)S(1)}, u32[]{:S(2)}) copy-start(f32[3072]{0:T(1024)S(1)} %select_add_fusion.13) | copy-start | bytes 36868 | tf_op jit(solution)/shard_map/while
  383.8 72.8 %copy-start.18 = (bf16[2,384,768]{2,1,0:T(8,128)(2,1)}, bf16[2,384,768]{2,1,0:T(8,128)(2,1)S(1)}, u32[]{:S(2)}) copy-start(bf16[2,384,768]{2,1,0:T(8,128)(2,1)S(1)} %fusion.233) | copy-start | bytes 3538948 | tf_op jit(solution)/shard_map/while
  547.5 31.9 %collective-permute-start.1 = (bf16[384,768]{1,0:T(8,128)(2,1)}, bf16[384,768]{1,0:T(8,128)(2,1)S(1)}, u32[]{:S(2)}, u32[]{:S(2)}) collective-permute-start(bf16[384,768]{1,0:T(8,128)(2,1)} %get-tuple-element.1910), channel_id=1, source_target_pairs={{8,0},{16,8},{24,16},{9,1},{17,9},{25,17},{10,2},{18,10},{26,18},{... | collective-permute-start | bytes 1769480 | tf_op jit(solution)/shard_map/while/body/eval_jaxpr/ppermute | solution.py:16
  552.5 26.9 %copy-start.10 = (bf16[2,384,768]{2,1,0:T(8,128)(2,1)S(1)}, bf16[2,384,768]{2,1,0:T(8,128)(2,1)}, u32[]{:S(2)}) copy-start(bf16[2,384,768]{2,1,0:T(8,128)(2,1)} %copy-done.9) | copy-start | bytes 3538948 | tf_op jit(solution)/shard_map/while
  552.5 26.9 %copy-start.24 = (f32[1,768]{1,0:T(1,128)S(1)}, f32[1,768]{1,0:T(1,128)}, u32[]{:S(2)}) copy-start(f32[1,768]{1,0:T(1,128)} %copy-done.23) | copy-start | bytes 9220 | tf_op jit(solution)/shard_map/while
  552.5 26.9 %copy-start.27 = (f32[1,768]{1,0:T(1,128)S(1)}, f32[1,768]{1,0:T(1,128)}, u32[]{:S(2)}) copy-start(f32[1,768]{1,0:T(1,128)} %copy-done.26) | copy-start | bytes 9220 | tf_op jit(solution)/shard_map/while
  670.3 30.3 %collective-permute-start.1 = (bf16[384,768]{1,0:T(8,128)(2,1)}, bf16[384,768]{1,0:T(8,128)(2,1)S(1)}, u32[]{:S(2)}, u32[]{:S(2)}) collective-permute-start(bf16[384,768]{1,0:T(8,128)(2,1)} %get-tuple-element.1910), channel_id=1, source_target_pairs={{8,0},{16,8},{24,16},{9,1},{17,9},{25,17},{10,2},{18,10},{26,18},{... | collective-permute-start | bytes 1769480 | tf_op jit(solution)/shard_map/while/body/eval_jaxpr/ppermute | solution.py:16
  675.3 26.3 %copy-start.10 = (bf16[2,384,768]{2,1,0:T(8,128)(2,1)S(1)}, bf16[2,384,768]{2,1,0:T(8,128)(2,1)}, u32[]{:S(2)}) copy-start(bf16[2,384,768]{2,1,0:T(8,128)(2,1)} %copy-done.9) | copy-start | bytes 3538948 | tf_op jit(solution)/shard_map/while
  675.3 26.3 %copy-start.24 = (f32[1,768]{1,0:T(1,128)S(1)}, f32[1,768]{1,0:T(1,128)}, u32[]{:S(2)}) copy-start(f32[1,768]{1,0:T(1,128)} %copy-done.23) | copy-start | bytes 9220 | tf_op jit(solution)/shard_map/while
  675.3 26.3 %copy-start.27 = (f32[1,768]{1,0:T(1,128)S(1)}, f32[1,768]{1,0:T(1,128)}, u32[]{:S(2)}) copy-start(f32[1,768]{1,0:T(1,128)} %copy-done.26) | copy-start | bytes 9220 | tf_op jit(solution)/shard_map/while
  1275.3 37.0 %collective-permute-start.3 = (bf16[768,1536]{1,0:T(8,128)(2,1)S(1)}, bf16[768,1536]{1,0:T(8,128)(2,1)}, u32[]{:S(2)}, u32[]{:S(2)}) collective-permute-start(bf16[768,1536]{1,0:T(8,128)(2,1)S(1)} %slice.388), channel_id=1, source_target_pairs={{8,0},{16,8},{24,16},{9,1},{17,9},{25,17},{10,2},{18,10},{26,18},{... | collective-permute-start | bytes 7077896 | tf_op jit(solution)/shard_map/ppermute | solution.py:16
  (113 other events, 640.6 us)
Sparse Core Ops, SparseCore 0:
  9.6 20.1 all-gather.2
  31.3 20.6 all-gather.4
  703.9 568.6 all-reduce.3
where the time goes:
time: 1340 us; the launch traced here: 1330 us
  waiting for transfers between devices  679 us (51%)
  other arithmetic  258 us (19%)
  local copies, waits for them, and re-layouts  133 us (10%)
  matrix products  104 us (8%)
  starting transfers between devices  78.6 us (6%)
  blocking collectives  35.7 us (3%)
  loops' own time  28 us (2%)
  between operations  14.2 us (1%)
    psum x1, waiting for transfers between devices, body(): lax.psum((grad_lead, grad_trail, grad_gain, grad_shift, grad_first, grad_...  569 us
    add x5, other arithmetic, backward_tick(): grad_trail = grad_trail + outcome[2]  102 us
    ppermute x12, starting transfers between devices, shifted(): return lax.ppermute(array, axis, pairs)  78.5 us
    ppermute x12, waiting for transfers between devices, shifted(): return lax.ppermute(array, axis, pairs)  74.4 us
    another operation x28, local copies, waits for them, and re-layouts  48.8 us
    another operation x26, other arithmetic  38 us
    psum x1, blocking collectives, body(): lax.psum((grad_lead, grad_trail, grad_gain, grad_shift, grad_first, grad_...  35.7 us
  transfers between devices with their start and end apart: 15, of which 5 were waited for; matrix products, arithmetic and copies ran while one was open for 12% of the time, Pallas kernels for 0%

commit v1 on v0

v1 whole, which is shorter than its diff:
```python
import jax
import jax.numpy as jnp
from jax import lax
from jax.experimental import pallas as pl
from jax.experimental.pallas import tpu as pltpu
from jax.sharding import PartitionSpec as P

D = 768
HEADS = 12
HEAD_DIM = 64
FF = 3072
L = 384
F32 = jnp.float32
BF = jnp.bfloat16
NT = (((1,), (1,)), ((), ()))
VM = pltpu.VMEM


def dot(a, b):
    return jnp.dot(a, b, preferred_element_type=F32)


def dot_nt(a, b):
    return lax.dot_general(a, b, NT, preferred_element_type=F32)


def norm_parts(x):
    center = x - jnp.mean(x, axis=-1, keepdims=True)
    inv = lax.rsqrt(jnp.mean(center * center, axis=-1, keepdims=True) + 1e-06)
    return center * inv, inv


def swap_halves(a):
    lane = lax.broadcasted_iota(jnp.int32, (1, 128), 1)
    first = (lane % 64) < 32
    out = []
    for i in range(a.shape[1] // 128):
        s = a[:, 128 * i : 128 * (i + 1)]
        out.append(jnp.where(first, pltpu.roll(s, 96, 1), pltpu.roll(s, 32, 1)))
    return jnp.concatenate(out, axis=1) if len(out) > 1 else out[0]


def pick(flag, want, own, oth, src, dst, sem):
    @pl.when(flag == want)
    def _():
        pltpu.make_async_copy(own.at[src], dst, sem).start()

    @pl.when(flag != want)
    def _():
        pltpu.make_async_copy(oth.at[src], dst, sem).start()


def cols(start, size):
    return (slice(None), pl.ds(start, size))


def attn_fwd_kernel(
    core, x_ref, own, oth, bias, second, gain, shift, cosf, sinf, segc, segr,
    out_ref, qkv_ref, pt_ref, ml_ref, n_ref, wbuf, vt, mlt, sems,
):
    c = core[0]
    for i in range(4):
        pick(c, 0, own, oth, cols(D * i, D), wbuf.at[i], sems.at[i])
    x = x_ref[...].astype(F32)
    xh, _ = norm_parts(x)
    n = (xh * gain[...] + shift[...]).astype(BF)
    n_ref[...] = n
    for i in range(3):
        pltpu.make_async_copy(own.at[cols(D * i, D)], wbuf.at[i], sems.at[i]).wait()
        part = dot(n, wbuf[i]) + bias[:, D * i : D * (i + 1)]
        if i < 2:
            part = part * cosf[...] + swap_halves(part) * sinf[...]
        part = part.astype(BF)
        if i == 0:
            part = part * BF(HEAD_DIM**-0.5)
        qkv_ref[:, D * i : D * (i + 1)] = part
    vt[...] = qkv_ref[:, 2 * D : 3 * D].T
    same = segc[...] == segr[...]
    lane = lax.broadcasted_iota(jnp.int32, (1, 128), 1)
    for p in range(HEADS // 2):
        qp = qkv_ref[:, 128 * p : 128 * (p + 1)]
        kp = qkv_ref[:, D + 128 * p : D + 128 * (p + 1)]
        for hh in range(2):
            h = 2 * p + hh
            km = jnp.where((lane // 64) == hh, kp, BF(0))
            st = dot_nt(km, qp)
            st = jnp.where(same, st, -1e30)
            e = jnp.exp(st - jnp.max(st, axis=0, keepdims=True))
            pt = (e * (1.0 / jnp.sum(e, axis=0, keepdims=True))).astype(BF)
            pt_ref[h] = pt
            mlt[64 * h : 64 * (h + 1), :] = dot(vt[64 * h : 64 * (h + 1), :], pt).astype(BF)
    ml = mlt[...].T
    ml_ref[...] = ml
    pltpu.make_async_copy(own.at[cols(3 * D, D)], wbuf.at[3], sems.at[3]).wait()
    out_ref[...] = (x + dot(ml, wbuf[3]) + second[...]).astype(BF)


def attn_bwd_kernel(
    core, x_ref, c_ref, own, oth, gain, shift, cosf, sinf, colp, rowp, qkv_ref, pt_ref, ml_ref,
    gx_ref, gp_ref, ggain, gshift, gbias, gfx, gfy, gsec, wbuf, kt, gm_ref, gqt, dsum, sems,
):
    c = core[0]
    for i in (3, 0, 1, 2):
        pick(c, 0, own, oth, cols(D * i, D), wbuf.at[i], sems.at[i])
    cw = c_ref[...]
    gsec[...] = jnp.sum(cw.astype(F32), axis=0, keepdims=True)
    kt[...] = qkv_ref[:, D : 2 * D].T
    pltpu.make_async_copy(own.at[cols(3 * D, D)], wbuf.at[3], sems.at[3]).wait()
    gm = dot_nt(cw, wbuf[3]).astype(BF)
    gm_ref[...] = gm
    prod = gm.astype(F32) * ml_ref[...].astype(F32)
    hi = prod.astype(BF)
    lo = (prod - hi.astype(F32)).astype(BF)
    hrow = lax.broadcasted_iota(jnp.int32, (16, D), 0)
    hcol = lax.broadcasted_iota(jnp.int32, (16, D), 1)
    sel = jnp.where(hcol // 64 == hrow, 1.0, 0.0).astype(BF)
    dsum[...] = dot_nt(sel, hi) + dot_nt(sel, lo)
    lane = lax.broadcasted_iota(jnp.int32, (1, 128), 1)
    fx = []
    fy = []
    for p in range(HEADS // 2):
        sl = slice(128 * p, 128 * (p + 1))
        qp = qkv_ref[:, sl]
        kp = qkv_ref[:, D + 128 * p : D + 128 * (p + 1)]
        vp = qkv_ref[:, 2 * D + 128 * p : 2 * D + 128 * (p + 1)]
        gmp = gm_ref[:, sl]
        gv = None
        for hh in range(2):
            h = 2 * p + hh
            here = (lane // 64) == hh
            pt = pt_ref[h]
            gpt = dot_nt(jnp.where(here, vp, BF(0)), gmp)
            gst = (pt.astype(F32) * (gpt - dsum[h : h + 1, :])).astype(BF)
            gvh = dot(pt, jnp.where(here, gmp, BF(0)))
            gkh = dot(gst, jnp.where(here, qp, BF(0)))
            gv = gvh if gv is None else gv + gvh
            gk = gkh if hh == 0 else gk + gkh
            gqt[64 * h : 64 * (h + 1), :] = dot(kt[64 * h : 64 * (h + 1), :], gst)
        gq = gqt[sl, :].T * (HEAD_DIM**-0.5)
        cs = cosf[:, sl]
        sn = sinf[:, sl]
        sq = swap_halves(gq)
        sk = swap_halves(gk)
        gqb = (gq * cs - sq * sn).astype(BF)
        gkb = (gk * cs - sk * sn).astype(BF)
        gvb = gv.astype(BF)
        gp_ref[:, sl] = gqb
        gp_ref[:, D + 128 * p : D + 128 * (p + 1)] = gkb
        gp_ref[:, 2 * D + 128 * p : 2 * D + 128 * (p + 1)] = gvb
        th = sq * (qp.astype(F32) * (HEAD_DIM**0.5)) + sk * kp.astype(F32)
        gfx[:, sl] = jnp.sum(th * colp[...], axis=0, keepdims=True)
        gfy[:, sl] = jnp.sum(th * rowp[...], axis=0, keepdims=True)
        for i, g in enumerate((gqb, gkb, gvb)):
            gbias[:, D * i + 128 * p : D * i + 128 * (p + 1)] = jnp.sum(
                g.astype(F32), axis=0, keepdims=True
            )
    gn = None
    for i in range(3):
        pltpu.make_async_copy(own.at[cols(D * i, D)], wbuf.at[i], sems.at[i]).wait()
        part = dot_nt(gp_ref[:, D * i : D * (i + 1)], wbuf[i])
        gn = part if gn is None else gn + part
    gx_ref[...] = norm_back(gn, x_ref, cw, gain, ggain, gshift)


def norm_back(gn, x_ref, cw, gain, ggain, gshift):
    xh, inv = norm_parts(x_ref[...].astype(F32))
    ggain[...] = jnp.sum(gn * xh, axis=0, keepdims=True)
    gshift[...] = jnp.sum(gn, axis=0, keepdims=True)
    u = gn * gain[...]
    gx = inv * (
        u
        - jnp.mean(u, axis=-1, keepdims=True)
        - xh * jnp.mean(u * xh, axis=-1, keepdims=True)
    )
    return (cw.astype(F32) + gx).astype(BF)


C0 = 0.7978845608028654
C1 = 0.044715


def mlp_load(c, own, oth, w1, wd, sems):
    for j in range(4):
        pick(c, 1, own, oth, cols(D * j, D), w1.at[j], sems.at[j])
        pick(c, 0 if j < 2 else 1, own, oth, cols(FF + D * (j % 2), D), wd.at[j], sems.at[4 + j])


def mlp_wait(own, w1, wd, sems, j):
    pltpu.make_async_copy(own.at[cols(D * j, D)], w1.at[j], sems.at[j]).wait()
    pltpu.make_async_copy(own.at[cols(FF + D * (j % 2), D)], wd.at[j], sems.at[4 + j]).wait()


def mlp_fwd_kernel(
    core, x_ref, own, oth, bias, second, gain, shift, out_ref, act_ref, dg_ref, n_ref, w1, wd, sems
):
    mlp_load(core[0], own, oth, w1, wd, sems)
    x = x_ref[...].astype(F32)
    xh, _ = norm_parts(x)
    n = (xh * gain[...] + shift[...]).astype(BF)
    n_ref[...] = n
    acc = x + second[...]
    for j in range(4):
        mlp_wait(own, w1, wd, sems, j)
        h = dot(n, w1[j]) + bias[:, D * j : D * (j + 1)]
        h2 = h * h
        t = jnp.tanh(C0 * (h + C1 * h * h2))
        half = 0.5 * (1.0 + t)
        act = (h * half).astype(BF)
        dg = half + (0.5 * C0) * h * (1.0 - t * t) * (1.0 + (3.0 * C1) * h2)
        act_ref[:, D * j : D * (j + 1)] = act
        dg_ref[:, D * j : D * (j + 1)] = dg.astype(BF)
        acc = acc + dot_nt(act, wd[j])
    out_ref[...] = acc.astype(BF)


def mlp_bwd_kernel(
    core, x_ref, c_ref, own, oth, gain, shift, dg_ref, gx_ref, gh_ref, ggain, gshift, gbias, gsec, w1, wd, sems
):
    mlp_load(core[0], own, oth, w1, wd, sems)
    cw = c_ref[...]
    gsec[...] = jnp.sum(cw.astype(F32), axis=0, keepdims=True)
    gn = None
    for j in range(4):
        mlp_wait(own, w1, wd, sems, j)
        ga = dot(cw, wd[j])
        gh = (ga * dg_ref[:, D * j : D * (j + 1)].astype(F32)).astype(BF)
        gh_ref[:, D * j : D * (j + 1)] = gh
        gbias[:, D * j : D * (j + 1)] = jnp.sum(gh.astype(F32), axis=0, keepdims=True)
        part = dot_nt(gh, w1[j])
        gn = part if gn is None else gn + part
    gx_ref[...] = norm_back(gn, x_ref, cw, gain, ggain, gshift)


SMEM = pl.BlockSpec(memory_space=pltpu.SMEM)
VS = pl.BlockSpec(memory_space=pltpu.VMEM)
ANY = pl.BlockSpec(memory_space=pl.ANY)
PARAMS = dict(vmem_limit_bytes=56 * 1024 * 1024)


def sds(shape, dtype=BF):
    return jax.ShapeDtypeStruct(shape, dtype)


def call(kernel, name, in_specs, outs, scratch, flops, nbytes):
    return pl.pallas_call(
        kernel,
        name=name,
        in_specs=in_specs,
        out_specs=[VS] * len(outs),
        out_shape=outs,
        scratch_shapes=scratch,
        compiler_params=pltpu.CompilerParams(**PARAMS),
        cost_estimate=pl.CostEstimate(flops=flops, bytes_accessed=nbytes, transcendentals=0),
    )


def attn_fwd(*a):
    return call(
        attn_fwd_kernel, "attn_fwd", [SMEM, VS, ANY, ANY] + [VS] * 8,
        [sds((L, D)), sds((L, 3 * D)), sds((HEADS, L, L)), sds((L, D)), sds((L, D))],
        [VM((4, D, D), BF), VM((D, L), BF), VM((D, L), BF), pltpu.SemaphoreType.DMA((4,))],
        int(4e9), int(12e6),
    )(*a)


def attn_bwd(*a):
    return call(
        attn_bwd_kernel, "attn_bwd", [SMEM, VS, VS, ANY, ANY] + [VS] * 9,
        [sds((L, D)), sds((L, 3 * D)), sds((1, D), F32), sds((1, D), F32), sds((1, 3 * D), F32),
         sds((1, D), F32), sds((1, D), F32), sds((1, D), F32)],
        [VM((4, D, D), BF), VM((D, L), BF), VM((L, D), BF), VM((D, L), F32), VM((16, L), F32),
         pltpu.SemaphoreType.DMA((4,))],
        int(6e9), int(12e6),
    )(*a)


def mlp_fwd(*a):
    return call(
        mlp_fwd_kernel, "mlp_fwd", [SMEM, VS, ANY, ANY] + [VS] * 4,
        [sds((L, D)), sds((L, FF)), sds((L, FF)), sds((L, D))],
        [VM((4, D, D), BF), VM((4, D, D), BF), pltpu.SemaphoreType.DMA((8,))],
        int(4e9), int(14e6),
    )(*a)


def mlp_bwd(*a):
    return call(
        mlp_bwd_kernel, "mlp_bwd", [SMEM, VS, VS, ANY, ANY] + [VS] * 3,
        [sds((L, D)), sds((L, FF)), sds((1, D), F32), sds((1, D), F32), sds((1, FF), F32), sds((1, D), F32)],
        [VM((4, D, D), BF), VM((4, D, D), BF), pltpu.SemaphoreType.DMA((8,))],
        int(4e9), int(14e6),
    )(*a)


def core_swap(a):
    return lax.ppermute(a, "section", [(0, 1), (1, 0), (2, 3), (3, 2)])


def layer_swap(a, pairs):
    return lax.ppermute(a, "section", pairs)


def layout(grid_rows):
    heights = grid_rows[:, 0]
    widths = grid_rows[:, 1]
    counts = heights * widths
    end_one = counts[0]
    end_two = end_one + counts[1]
    places = jnp.arange(L, dtype=jnp.int32)
    segment = (places >= end_one).astype(jnp.int32) + (places >= end_two).astype(jnp.int32)
    offset = jnp.where(segment == 0, 0, end_one)
    across = jnp.where(segment == 0, widths[0], widths[1])
    inside = places - offset
    row_pos = jnp.where(segment < 2, inside // across, 0).astype(F32)
    col_pos = jnp.where(segment < 2, inside % across, 0).astype(F32)
    return segment, row_pos, col_pos


def ring_order(n):
    return list(range(0, n, 2)) + list(range(n - 1, 0, -2))


class Ring:
    def __init__(self, array, direction, n, place):
        self.array, self.n, self.place, self.d = array, n, place, direction
        self.r = array.shape[0] // n
        order = ring_order(n)
        self.pairs = [(order[i], order[(i + direction) % n]) for i in range(n)]
        self.cur = self.own(0)
        self.shards = []

    def index(self, t):
        return (self.place - self.d * t) % self.n

    def own(self, t):
        return lax.dynamic_slice_in_dim(self.array, self.index(t) * self.r, self.r, 0)

    def step(self, t):
        got = lax.ppermute(self.cur, "dp", self.pairs)
        if t < self.n - 1:
            self.cur = got + self.own(t + 1)
            if t == self.n - 2:
                self.shards.append((self.index(-1), self.cur))
        else:
            self.cur = got
            self.shards.append((self.index(t - self.n + 1), got))

    def total(self):
        out = jnp.zeros_like(self.array)
        for index, shard in self.shards:
            out = lax.dynamic_update_slice_in_dim(out, shard, index * self.r, 0)
        return out


def all_reduce(arrays):
    n = lax.axis_size("dp")
    if n > 16:
        return [lax.psum(a, "dp") for a in arrays]
    i = lax.axis_index("dp")
    place = jnp.where(i % 2 == 0, i // 2, n - 1 - i // 2)
    rings = []
    for a in arrays:
        half = a.shape[0] // 2
        rings.append((Ring(a[:half], 1, n, place), Ring(a[half:], -1, n, place)))
    for t in range(2 * n - 2):
        for pair in rings:
            for ring in pair:
                ring.step(t)
    return [jnp.concatenate([up.total(), down.total()], axis=0) for up, down in rings]


def gram(a, b):
    return lax.dot_general(a, b, (((0,), (0,)), ((), ())), preferred_element_type=F32)


def body(
    block_input, cotangent, grid_sizes, section_weight, norm_gain, norm_bias, first_vector, second_vector
):
    section = lax.axis_index("section")
    core = section % 2
    layer = section // 2
    flag = jnp.full((1,), core, jnp.int32)
    first_core = core == 0
    first_layer = layer == 0

    own = section_weight[0]
    oth = core_swap(own)
    vec = jnp.concatenate([norm_gain[0], norm_bias[0], first_vector[0], second_vector[0]])[None]
    vec_oth = core_swap(vec)
    vec_a = jnp.where(first_core, vec, vec_oth)
    vec_m = jnp.where(first_core, vec_oth, vec)

    def split(v):
        return v[:, :D], v[:, D : 2 * D], v[:, 2 * D : 2 * D + FF], v[:, 2 * D + FF :]

    gain_a, shift_a, first_a, second_a = split(vec_a)
    gain_m, shift_m, first_m, second_m = split(vec_m)

    def half_row(block):
        rows = block.reshape(2, L, -1)
        mine = lax.dynamic_index_in_dim(rows, core, 0, keepdims=False)
        send = lax.dynamic_index_in_dim(rows, 1 - core, 0, keepdims=False)
        return mine, send

    x_mine, x_send = half_row(block_input)
    c_mine, c_send = half_row(cotangent)
    got = core_swap(jnp.concatenate([x_send, c_send], axis=1))
    quarter = x_mine.shape[1]

    def in_order(pick_first, a, b):
        return jnp.where(pick_first, jnp.concatenate([a, b], axis=1), jnp.concatenate([b, a], axis=1))

    x_half = in_order(first_core, x_mine, got[:, :quarter])
    c_half = in_order(first_core, c_mine, got[:, quarter:])
    got = layer_swap(jnp.where(first_layer, c_half, x_half), [(0, 2), (1, 3), (2, 0), (3, 1)])
    field = in_order(first_layer, jnp.where(first_layer, x_half, c_half), got)

    segment, row_pos, col_pos = layout(lax.dynamic_index_in_dim(grid_sizes, core, 0, keepdims=False))

    def lanes(freq):
        by_head = freq.reshape(HEADS, 1, HEAD_DIM // 2)
        return jnp.broadcast_to(by_head, (HEADS, 2, HEAD_DIM // 2)).reshape(1, D)

    freq_x = lanes(first_a[0, 3 * D : 3 * D + D // 2])
    freq_y = lanes(first_a[0, 3 * D + D // 2 :])
    theta = col_pos[:, None] * freq_x + row_pos[:, None] * freq_y
    sign = jnp.where(jnp.arange(D) % HEAD_DIM < HEAD_DIM // 2, -1.0, 1.0).astype(F32)
    cosf = jnp.cos(theta)
    sinf = jnp.sin(theta) * sign
    segc, segr = segment[:, None], segment[None, :]
    colp, rowp = col_pos[:, None], row_pos[:, None]

    def attn_f(x):
        return attn_fwd(
            flag, x, own, oth, first_a[:, : 3 * D], second_a, gain_a, shift_a, cosf, sinf, segc, segr
        )

    def mlp_f(x):
        return mlp_fwd(flag, x, own, oth, first_m, second_m, gain_m, shift_m)

    x_one = mlp_f(attn_f(field)[0])[0]
    arrived = layer_swap(x_one, [(0, 2), (1, 3)])
    x_in = jnp.where(first_layer, field, arrived)
    x_mid, qkv, pt, ml, n_a = attn_f(x_in)
    x_out, act, dg, n_m = mlp_f(x_mid)

    def backward(c_out):
        mlp = mlp_bwd(flag, x_mid, c_out, own, oth, gain_m, shift_m, dg)
        attn = attn_bwd(
            flag, x_in, mlp[0], own, oth, gain_a, shift_a, cosf, sinf, colp, rowp, qkv, pt, ml
        )
        return mlp, attn

    c_one = backward(field)[1][0]
    arrived = layer_swap(c_one, [(2, 0), (3, 1)])
    c_out = jnp.where(first_layer, arrived, field)
    mlp, attn = backward(c_out)
    c_mid, gh, ggain_m, gshift_m, gbias_m, gsec_m = mlp
    c_in, gp, ggain_a, gshift_a, gbias_a, gfx, gfy, gsec_a = attn

    def half(array, start, size, which):
        return lax.dynamic_slice_in_dim(array, start + which * size, size, 1)

    def pair(array, groups):
        size = array.shape[1] // groups // 2
        mine = [half(array, 2 * size * g, size, core) for g in range(groups)]
        send = [half(array, 2 * size * g, size, 1 - core) for g in range(groups)]
        mine, send = (jnp.concatenate(p, axis=1) if groups > 1 else p[0] for p in (mine, send))
        return jnp.concatenate([mine, core_swap(send)], axis=0)

    def both(array):
        return jnp.concatenate([array, core_swap(array)], axis=0)

    down_grad = gram(both(c_out), pair(act, 1)).astype(BF)
    up_grad = gram(both(n_m), pair(gh, 1)).astype(BF)
    qkv_grad = gram(both(n_a), pair(gp, 3)).astype(BF)
    out_grad = gram(both(ml), pair(c_mid, 1)).astype(BF)

    mlp_sum, attn_sum = all_reduce(
        [jnp.concatenate([down_grad, up_grad], axis=1), jnp.concatenate([qkv_grad, out_grad], axis=1)]
    )
    down_sum, up_sum = mlp_sum[:, : FF // 2], mlp_sum[:, FF // 2 :]
    other = core_swap(jnp.where(first_core, up_sum, attn_sum))
    h = D // 2

    def woven(a, b):
        return jnp.concatenate([p[:, h * g : h * (g + 1)] for g in range(4) for p in (a, b)], axis=1)

    lead = jnp.where(first_core, woven(attn_sum, other), jnp.concatenate([other, up_sum], axis=1))
    weight_grad = jnp.concatenate([lead, down_sum], axis=1).astype(F32)

    def fold(v):
        pairs = v.reshape(HEADS, 2, HEAD_DIM // 2)
        return (pairs[:, 0] - pairs[:, 1]).reshape(1, -1)

    vg_a = jnp.concatenate([ggain_a, gshift_a, gbias_a, fold(gfx), fold(gfy), gsec_a], axis=1)
    vg_m = jnp.concatenate([ggain_m, gshift_m, gbias_m, gsec_m], axis=1)
    vg = jnp.where(first_core, vg_a, vg_m) + core_swap(jnp.where(first_core, vg_m, vg_a))
    vg = lax.psum(vg, "dp")
    vgain, vshift, vfirst, vsecond = split(vg)

    def rows_of(attn_row, mlp_row):
        got = core_swap(jnp.where(first_core, mlp_row, attn_row))
        return jnp.where(
            first_core,
            jnp.concatenate([attn_row, got], axis=0),
            jnp.concatenate([got, mlp_row], axis=0),
        )[None]

    return (
        rows_of(x_mid, x_out),
        rows_of(c_in, c_mid),
        weight_grad[None],
        vgain,
        vshift,
        vfirst,
        vsecond,
    )


def solution(mesh):
    in_specs = (
        P("dp", "section"),
        P("dp", "section"),
        P("dp", None, None),
        P("section", None, None),
        P("section", None),
        P("section", None),
        P("section", None),
        P("section", None),
    )
    out_specs = (
        P("section", "dp", None),
        P("section", "dp", None),
        P("section", None, None),
        P("section", None),
        P("section", None),
        P("section", None),
        P("section", None),
    )
    return jax.shard_map(body, mesh=mesh, in_specs=in_specs, out_specs=out_specs, check_vma=False)
```

time: 1340 us -> 415 us (0.31)
  waiting for transfers between devices: 679 us -> 113 us
  other arithmetic: 258 us -> 50.1 us
  local copies, waits for them, and re-layouts: 133 us -> 22.3 us
  Pallas kernels: 0 us -> 102 us
  matrix products: 104 us -> 12.1 us
  loops' own time: 28 us -> 0 us
    psum x1 -> x0, waiting for transfers between devices: 569 us -> none  [body(): lax.psum((grad_lead, grad_trail, grad_gain, grad_shift, grad_first, grad_...]
    add x22 -> x27, other arithmetic: 124 us -> 3.87 us  [the longest x2 2.43 us: layout(): (places >= end_one).astype(jnp.int32)]
    pallas_call x0 -> x8, Pallas kernels: none -> 102 us  [the longest x2 30.8 us: attn_bwd(): call(attn_bwd_kernel, 'attn_bwd', [SMEM, VS, VS, ANY, ANY] + [VS] * 9, [s...]
    dot_general x30 -> x4, matrix products: 76.9 us -> 12.1 us  [gram(): lax.dot_general(a, b, (((0,), (0,)), ((), ())), preferred_element_type=F32)]
    another operation x28 -> x4, local copies, waits for them, and re-layouts: 48.8 us -> 0.7 us
    ppermute x12 -> x74, waiting for transfers between devices: 74.4 us -> 113 us  [the longest x56 93.7 us: step(): got = lax.ppermute(self.cur, 'dp', self.pairs)]
    another operation x26 -> x0, other arithmetic: 38 us -> none
    all_gather x2 -> x0, waiting for transfers between devices: 34.9 us -> none  [the longest x1 19.9 us: body(): lax.all_gather(cotangent, 'section', axis=1, tiled=True)]
  transfers between devices with their start and end apart: 15 -> 74, of which waited for: 5 -> 32; matrix products, arithmetic and copies ran while one was open for 12% -> 16% of each run, Pallas kernels for 0% -> 6%
where the time goes in v1:
time: 415 us; the launch traced here: 411 us
  waiting for transfers between devices  113 us (27%)
  Pallas kernels  102 us (25%)
  starting transfers between devices  71.4 us (17%)
  other arithmetic  50.1 us (12%)
  blocking collectives  36.7 us (9%)
  local copies, waits for them, and re-layouts  22.3 us (5%)
  matrix products  12.1 us (3%)
    ppermute x56, waiting for transfers between devices, step(): got = lax.ppermute(self.cur, 'dp', self.pairs)  93.7 us
    ppermute x56, starting transfers between devices, step(): got = lax.ppermute(self.cur, 'dp', self.pairs)  59.4 us
    psum x1, blocking collectives, body(): vg = lax.psum(vg, 'dp')  36.7 us
    pallas_call x2, Pallas kernels, attn_bwd(): call(attn_bwd_kernel, 'attn_bwd', [SMEM, VS, VS, ANY, ANY] + [VS] * 9, [s...  30.8 us
    pallas_call x2, Pallas kernels, attn_fwd(): call(attn_fwd_kernel, 'attn_fwd', [SMEM, VS, ANY, ANY] + [VS] * 8, [sds((...  28 us
    pallas_call x2, Pallas kernels, mlp_fwd(): call(mlp_fwd_kernel, 'mlp_fwd', [SMEM, VS, ANY, ANY] + [VS] * 4, [sds((L,...  22.4 us
    pallas_call x2, Pallas kernels, mlp_bwd(): call(mlp_bwd_kernel, 'mlp_bwd', [SMEM, VS, VS, ANY, ANY] + [VS] * 3, [sds...  20.6 us
    ppermute x3, waiting for transfers between devices, layer_swap(): return lax.ppermute(a, 'section', pairs)  16.9 us
  transfers between devices with their start and end apart: 74, of which 32 were waited for; matrix products, arithmetic and copies ran while one was open for 16% of the time, Pallas kernels for 6%

profile of v1, /device:TPU:0, one launch (start us, length us, event | category | flops | bytes accessed | tf_op | source)
XLA Modules:
  0.0 411.3 jit_solution(9608208437601687609)
XLA Ops:
  18.4 5.7 %sine_multiply_fusion = (f32[384,768]{1,0:T(8,128)}, f32[384,768]{1,0:T(8,128)}) fusion(f32[768]{0:T(1024)S(1)} %fusion.93, f32[768]{0:T(1024)S(1)} %mul.67, f32[384]{0:T(512)S(1)} %get-tuple-element.116, f32[768]{0:T(1024)S(1)} %mul.63, f32[384]{0:T(512)S(1)} %get-tuple-element.115), kind=kLoop, calls=%fused_computation.63 | loop fusion | flops 1179648 | bytes 2371584 | tf_op jit(solution)/shard_map/mul | solution.py:429
  25.1 14.0 %attn_fwd.2 = (bf16[384,768]{1,0:T(8,128)(2,1)}, bf16[384,2304]{1,0:T(8,128)(2,1)}, bf16[12,384,384]{2,1,0:T(8,128)(2,1)}, bf16[384,768]{1,0:T(8,128)(2,1)}, bf16[384,768]{1,0:T(8,128)(2,1)}) custom-call(s32[1]{0:T(128)} %bitcast.core, bf16[384,768]{1,0:T(8,128)(2,1)} %maximum_select_fusion.3.x_ref.c_ref, bf16[768,4608]{1,0:T(8,128)(2,1)} %bitcast.34, ...), custom_call_target="tpu_custom_call" | custom-call | flops 4000000000 | bytes 12000000 | tf_op jit(solution)/shard_map/attn_fwd/pallas_call | solution.py:258
  39.1 11.4 %mlp_fwd.2 = (bf16[384,768]{1,0:T(8,128)(2,1)}, bf16[384,3072]{1,0:T(8,128)(2,1)}, bf16[384,3072]{1,0:T(8,128)(2,1)}, bf16[384,768]{1,0:T(8,128)(2,1)}) custom-call(s32[1]{0:T(128)} %bitcast.core, bf16[384,768]{1,0:T(8,128)(2,1)} %get-tuple-element.34.x_ref, bf16[768,4608]{1,0:T(8,128)(2,1)} %bitcast.35, bf16[768,4608]{1,0:T(8,128)(2,1)} %collective-permute-done.2.oth, ...), custom_call_target="tpu_custom_call" | custom-call | flops 4000000000 | bytes 14000000 | tf_op jit(solution)/shard_map/mlp_fwd/pallas_call | solution.py:278
  50.5 3.7 collective-permute-start.4
  54.2 6.5 %fusion.61 = (f32[384,1]{1,0:T(8,128)}, f32[384,1]{1,0:T(8,128)}) fusion(s32[]{:T(128)} %bitcast.11, s32[]{:T(128)} %bitcast.10, s32[]{:T(128)S(6)} %add.433, s32[]{:T(128)} %bitcast.8), kind=kLoop, calls=%fused_computation.139 | loop fusion | flops 12672 | bytes 3088 | tf_op jit(solution)/shard_map/convert_element_type | solution.py:315
  60.7 5.8 %collective-permute-done.4 = bf16[384,768]{1,0:T(8,128)(2,1)S(1)} collective-permute-done((bf16[384,768]{1,0:T(8,128)(2,1)}, bf16[384,768]{1,0:T(8,128)(2,1)S(1)}, u32[]{:S(2)}, u32[]{:S(2)}) %collective-permute-start.4) | collective-permute-done | bytes 589856 | tf_op jit(solution)/shard_map/ppermute | solution.py:300
  67.6 14.0 %attn_fwd.3 = (bf16[384,768]{1,0:T(8,128)(2,1)}, bf16[384,2304]{1,0:T(8,128)(2,1)}, bf16[12,384,384]{2,1,0:T(8,128)(2,1)}, bf16[384,768]{1,0:T(8,128)(2,1)}, bf16[384,768]{1,0:T(8,128)(2,1)}) custom-call(s32[1]{0:T(128)} %bitcast.core, bf16[384,768]{1,0:T(8,128)(2,1)} %broadcast_select_fusion.3.x_ref, bf16[768,4608]{1,0:T(8,128)(2,1)} %bitcast.36, ...), custom_call_target="tpu_custom_call" | custom-call | flops 4000000000 | bytes 12000000 | tf_op jit(solution)/shard_map/attn_fwd/pallas_call | solution.py:258
  81.6 11.0 %mlp_fwd.3 = (bf16[384,768]{1,0:T(8,128)(2,1)}, bf16[384,3072]{1,0:T(8,128)(2,1)}, bf16[384,3072]{1,0:T(8,128)(2,1)}, bf16[384,768]{1,0:T(8,128)(2,1)}) custom-call(s32[1]{0:T(128)} %bitcast.core, bf16[384,768]{1,0:T(8,128)(2,1)} %get-tuple-element.36.x_ref, bf16[768,4608]{1,0:T(8,128)(2,1)} %bitcast.37, bf16[768,4608]{1,0:T(8,128)(2,1)} %collective-permute-done.2.oth, ...), custom_call_target="tpu_custom_call" | custom-call | flops 4000000000 | bytes 14000000 | tf_op jit(solution)/shard_map/mlp_fwd/pallas_call | solution.py:278
  92.6 10.3 %mlp_bwd.2 = (bf16[384,768]{1,0:T(8,128)(2,1)}, bf16[384,3072]{1,0:T(8,128)(2,1)}, f32[1,768]{1,0:T(1,128)}, f32[1,768]{1,0:T(1,128)}, f32[1,3072]{1,0:T(1,128)}, /*index=5*/f32[1,768]{1,0:T(1,128)}) custom-call(s32[1]{0:T(128)} %bitcast.core, bf16[384,768]{1,0:T(8,128)(2,1)} %get-tuple-element.36.x_ref, bf16[384,768]{1,0:T(8,128)(2,1)} %maximum_select_fusion.3.x_ref.c_ref, ...), custom_call_target="tpu_custom_call" | custom-call | flops 4000000000 | bytes 14000000 | tf_op jit(solution)/shard_map/mlp_bwd/pallas_call | solution.py:287
  103.0 15.6 %attn_bwd.2 = (bf16[384,768]{1,0:T(8,128)(2,1)}, bf16[384,2304]{1,0:T(8,128)(2,1)}, f32[1,768]{1,0:T(1,128)}, f32[1,768]{1,0:T(1,128)}, f32[1,2304]{1,0:T(1,128)...) custom-call(s32[1]{0:T(128)} %bitcast.core, bf16[384,768]{1,0:T(8,128)(2,1)} %broadcast_select_fusion.3.x_ref, ...), custom_call_target="tpu_custom_call" | custom-call | flops 6000000000 | bytes 12000000 | tf_op jit(solution)/shard_map/attn_bwd/pallas_call | solution.py:267
  123.4 11.0 %collective-permute-done.6 = bf16[384,768]{1,0:T(8,128)(2,1)} collective-permute-done((bf16[384,768]{1,0:T(8,128)(2,1)}, bf16[384,768]{1,0:T(8,128)(2,1)}, u32[]{:S(2)}, u32[]{:S(2)}) %collective-permute-start.6) | collective-permute-done | bytes 589856 | tf_op jit(solution)/shard_map/ppermute | solution.py:300
  136.5 10.3 %mlp_bwd.3 = (bf16[384,768]{1,0:T(8,128)(2,1)}, bf16[384,3072]{1,0:T(8,128)(2,1)}, f32[1,768]{1,0:T(1,128)}, f32[1,768]{1,0:T(1,128)}, f32[1,3072]{1,0:T(1,128)}, /*index=5*/f32[1,768]{1,0:T(1,128)}) custom-call(s32[1]{0:T(128)} %bitcast.core, bf16[384,768]{1,0:T(8,128)(2,1)} %get-tuple-element.36.x_ref, bf16[384,768]{1,0:T(8,128)(2,1)} %copy-done.6, ...), custom_call_target="tpu_custom_call" | custom-call | flops 4000000000 | bytes 14000000 | tf_op jit(solution)/shard_map/mlp_bwd/pallas_call | solution.py:287
  146.9 15.2 %attn_bwd.3 = (bf16[384,768]{1,0:T(8,128)(2,1)}, bf16[384,2304]{1,0:T(8,128)(2,1)}, f32[1,768]{1,0:T(1,128)}, f32[1,768]{1,0:T(1,128)}, f32[1,2304]{1,0:T(1,128)...) custom-call(s32[1]{0:T(128)} %bitcast.core, bf16[384,768]{1,0:T(8,128)(2,1)} %broadcast_select_fusion.3.x_ref, ...), custom_call_target="tpu_custom_call" | custom-call | flops 6000000000 | bytes 12000000 | tf_op jit(solution)/shard_map/attn_bwd/pallas_call | solution.py:267
  175.0 3.5 convolution_convert_fusion.1
  184.1 4.1 collective-permute-done.12
  203.0 5.4 %collective-permute-done.15 = bf16[48,1536]{1,0:T(8,128)(2,1)S(1)} collective-permute-done((bf16[48,1536]{1,0:T(8,128)(2,1)S(1)}, bf16[48,1536]{1,0:T(8,128)(2,1)S(1)}, u32[]{:S(2)}, u32[]{:S(2)}) %collective-permute-start.15) | collective-permute-done | bytes 147488 | tf_op jit(solution)/shard_map/ppermute | solution.py:339
  217.5 4.7 %collective-permute-done.17 = bf16[48,1536]{1,0:T(8,128)(2,1)S(1)} collective-permute-done((bf16[48,1536]{1,0:T(8,128)(2,1)S(1)}, bf16[48,1536]{1,0:T(8,128)(2,1)S(1)}, u32[]{:S(2)}, u32[]{:S(2)}) %collective-permute-start.17) | collective-permute-done | bytes 147488 | tf_op jit(solution)/shard_map/ppermute | solution.py:339
  231.4 3.9 collective-permute-done.46
  240.6 5.2 %collective-permute-done.20 = bf16[48,1536]{1,0:T(8,128)(2,1)S(1)} collective-permute-done((bf16[48,1536]{1,0:T(8,128)(2,1)S(1)}, bf16[48,1536]{1,0:T(8,128)(2,1)S(1)}, u32[]{:S(2)}, u32[]{:S(2)}) %collective-permute-start.20) | collective-permute-done | bytes 147488 | tf_op jit(solution)/shard_map/ppermute | solution.py:339
  254.7 4.6 %collective-permute-done.22 = bf16[48,1536]{1,0:T(8,128)(2,1)S(1)} collective-permute-done((bf16[48,1536]{1,0:T(8,128)(2,1)S(1)}, bf16[48,1536]{1,0:T(8,128)(2,1)S(1)}, u32[]{:S(2)}, u32[]{:S(2)}) %collective-permute-start.22) | collective-permute-done | bytes 147488 | tf_op jit(solution)/shard_map/ppermute | solution.py:339
  267.5 5.3 %collective-permute-done.24 = bf16[48,1536]{1,0:T(8,128)(2,1)S(1)} collective-permute-done((bf16[48,1536]{1,0:T(8,128)(2,1)S(1)}, bf16[48,1536]{1,0:T(8,128)(2,1)S(1)}, u32[]{:S(2)}, u32[]{:S(2)}) %collective-permute-start.24) | collective-permute-done | bytes 147488 | tf_op jit(solution)/shard_map/ppermute | solution.py:339
  279.8 4.5 %collective-permute-done.50 = bf16[48,3072]{1,0:T(8,128)(2,1)S(1)} collective-permute-done((bf16[48,3072]{1,0:T(8,128)(2,1)S(1)}, bf16[48,3072]{1,0:T(8,128)(2,1)S(1)}, u32[]{:S(2)}, u32[]{:S(2)}) %collective-permute-start.50) | collective-permute-done | bytes 294944 | tf_op jit(solution)/shard_map/ppermute | solution.py:339
  287.1 5.5 %collective-permute-done.51 = bf16[48,3072]{1,0:T(8,128)(2,1)S(1)} collective-permute-done((bf16[48,3072]{1,0:T(8,128)(2,1)S(1)}, bf16[48,3072]{1,0:T(8,128)(2,1)S(1)}, u32[]{:S(2)}, u32[]{:S(2)}) %collective-permute-start.51) | collective-permute-done | bytes 294944 | tf_op jit(solution)/shard_map/ppermute | solution.py:339
  294.7 5.0 %collective-permute-done.52 = bf16[48,3072]{1,0:T(8,128)(2,1)S(1)} collective-permute-done((bf16[48,3072]{1,0:T(8,128)(2,1)S(1)}, bf16[48,3072]{1,0:T(8,128)(2,1)S(1)}, u32[]{:S(2)}, u32[]{:S(2)}) %collective-permute-start.52) | collective-permute-done | bytes 294944 | tf_op jit(solution)/shard_map/ppermute | solution.py:339
  301.9 5.8 %collective-permute-done.53 = bf16[48,3072]{1,0:T(8,128)(2,1)S(1)} collective-permute-done((bf16[48,3072]{1,0:T(8,128)(2,1)S(1)}, bf16[48,3072]{1,0:T(8,128)(2,1)S(1)}, u32[]{:S(2)}, u32[]{:S(2)}) %collective-permute-start.53) | collective-permute-done | bytes 294944 | tf_op jit(solution)/shard_map/ppermute | solution.py:339
  310.0 6.8 %collective-permute-done.54 = bf16[48,3072]{1,0:T(8,128)(2,1)S(1)} collective-permute-done((bf16[48,3072]{1,0:T(8,128)(2,1)S(1)}, bf16[48,3072]{1,0:T(8,128)(2,1)S(1)}, u32[]{:S(2)}, u32[]{:S(2)}) %collective-permute-start.54) | collective-permute-done | bytes 294944 | tf_op jit(solution)/shard_map/ppermute | solution.py:339
  319.2 7.5 %collective-permute-done.55 = bf16[48,3072]{1,0:T(8,128)(2,1)S(1)} collective-permute-done((bf16[48,3072]{1,0:T(8,128)(2,1)S(1)}, bf16[48,3072]{1,0:T(8,128)(2,1)S(1)}, u32[]{:S(2)}, u32[]{:S(2)}) %collective-permute-start.55) | collective-permute-done | bytes 294944 | tf_op jit(solution)/shard_map/ppermute | solution.py:339
  328.8 4.6 %collective-permute-done.56 = bf16[48,3072]{1,0:T(8,128)(2,1)S(1)} collective-permute-done((bf16[48,3072]{1,0:T(8,128)(2,1)S(1)}, bf16[48,3072]{1,0:T(8,128)(2,1)S(1)}, u32[]{:S(2)}, u32[]{:S(2)}) %collective-permute-start.56) | collective-permute-done | bytes 294944 | tf_op jit(solution)/shard_map/ppermute | solution.py:339
  335.5 4.6 %collective-permute-done.57 = bf16[48,3072]{1,0:T(8,128)(2,1)S(1)} collective-permute-done((bf16[48,3072]{1,0:T(8,128)(2,1)S(1)}, bf16[48,3072]{1,0:T(8,128)(2,1)S(1)}, u32[]{:S(2)}, u32[]{:S(2)}) %collective-permute-start.57) | collective-permute-done | bytes 294944 | tf_op jit(solution)/shard_map/ppermute | solution.py:339
  341.9 6.7 %fusion.1 = (bf16[768,1536]{1,0:T(8,128)(2,1)}, bf16[768,1536]{1,0:T(8,128)(2,1)}, bf16[1,768,1536]{2,1,0:T(8,128)(2,1)}) fusion(bf16[384,1536]{1,0:T(8,128)(2,1)S(1)} %constant_dynamic-update-slice_fusion.26, bf16[384,1536]{1,0:T(8,128)(2,1)S(1)} %constant_dynamic-update-slice_fusion.34, pred[]{:T(512)S(6)} %eq.111, ...), kind=kLoop, calls=%fused_computation.19 | loop fusion | flops 15335424 | bytes 14155777 | tf_op jit(solution)/shard_map/jit(_where)/select_n | solution.py:483
  352.9 36.7 %psum.7 = f32[1,5376]{1,0:T(1,128)S(1)} all-reduce(f32[1,5376]{1,0:T(1,128)S(1)} %fusion.88), channel_id=1, replica_groups=mesh['section'=4,'dp'=8] {'dp'}, use_global_device_ids=true, to_apply=%region_0.1 | all-reduce | flops 5376 | bytes 43008 | tf_op jit(solution)/shard_map/psum | solution.py:499
  402.2 8.9 %maximum_convert_fusion = f32[1,768,4608]{2,1,0:T(8,128)} fusion(bf16[1,768,1536]{2,1,0:T(8,128)(2,1)} %get-tuple-element.73, bf16[1,768,3072]{2,1,0:T(8,128)(2,1)S(1)} %fusion), kind=kLoop, calls=%fused_computation | loop fusion | flops 14155776 | bytes 21233664 | tf_op jit(solution)/shard_map/convert_element_type | solution.py:490
  (345 shorter events, 139.9 us)
Async XLA Ops:
  0.7 24.4 %collective-permute-start.2 = (bf16[768,4608]{1,0:T(8,128)(2,1)}, bf16[768,4608]{1,0:T(8,128)(2,1)}, u32[]{:S(2)}, u32[]{:S(2)}) collective-permute-start(bf16[768,4608]{1,0:T(8,128)(2,1)} %bitcast.33), channel_id=1, source_target_pairs={{0,8},{8,0},{16,24},{24,16},{1,9},{9,1},{17,25},{25,17},{2,10},{10... | collective-permute-start | bytes 21233672 | tf_op jit(solution)/shard_map/ppermute | solution.py:296
  3.7 9.5 %collective-permute-start = (bf16[384,384]{1,0:T(8,128)(2,1)S(1)}, bf16[384,384]{1,0:T(8,128)(2,1)S(1)}, u32[]{:S(2)}, u32[]{:S(2)}) collective-permute-start(bf16[384,384]{1,0:T(8,128)(2,1)S(1)} %pad_maximum_fusion.3), channel_id=1, source_target_pairs={{0,8},{8,0},{16,24},{24,16},{1,9},{9,1},{17,25},{25,17},{2,10},{10... | collective-permute-start | bytes 884744 | tf_op jit(solution)/shard_map/ppermute | solution.py:296
  13.8 10.3 %collective-permute-start.1 = (bf16[384,384]{1,0:T(8,128)(2,1)S(1)}, bf16[384,384]{1,0:T(8,128)(2,1)S(1)}, u32[]{:S(2)}, u32[]{:S(2)}) collective-permute-start(bf16[384,384]{1,0:T(8,128)(2,1)S(1)} %get-tuple-element.85), channel_id=1, source_target_pairs={{0,16},{8,24},{16,0},{24,8},{1,17},{9,25},{17,1},{25,9},{2,18},{10... | collective-permute-start | bytes 884744 | tf_op jit(solution)/shard_map/ppermute | solution.py:300
  50.5 16.0 %collective-permute-start.4 = (bf16[384,768]{1,0:T(8,128)(2,1)}, bf16[384,768]{1,0:T(8,128)(2,1)S(1)}, u32[]{:S(2)}, u32[]{:S(2)}) collective-permute-start(bf16[384,768]{1,0:T(8,128)(2,1)} %get-tuple-element.35), channel_id=1, source_target_pairs={{0,16},{8,24},{1,17},{9,25},{2,18},{10,26},{3,19},{11,27},{4,20},{... | collective-permute-start | bytes 1769480 | tf_op jit(solution)/shard_map/ppermute | solution.py:300
  118.6 15.8 %collective-permute-start.6 = (bf16[384,768]{1,0:T(8,128)(2,1)}, bf16[384,768]{1,0:T(8,128)(2,1)}, u32[]{:S(2)}, u32[]{:S(2)}) collective-permute-start(bf16[384,768]{1,0:T(8,128)(2,1)} %get-tuple-element.43), channel_id=1, source_target_pairs={{16,0},{24,8},{17,1},{25,9},{18,2},{26,10},{19,3},{27,11},{20,4},{... | collective-permute-start | bytes 1769480 | tf_op jit(solution)/shard_map/ppermute | solution.py:300
  120.3 50.8 %collective-permute-start.10 = (bf16[384,768]{1,0:T(8,128)(2,1)}, bf16[384,768]{1,0:T(8,128)(2,1)}, u32[]{:S(2)}, u32[]{:S(2)}) collective-permute-start(bf16[384,768]{1,0:T(8,128)(2,1)} %get-tuple-element.42.ml_ref), channel_id=1, source_target_pairs={{0,8},{8,0},{16,24},{24,16},{1,9},{9,1},{17,25},{25,17},{2,10},{10... | collective-permute-start | bytes 1769480 | tf_op jit(solution)/shard_map/ppermute | solution.py:296
  122.0 52.3 %collective-permute-start.41 = (bf16[384,1536]{1,0:T(8,128)(2,1)}, bf16[384,1536]{1,0:T(8,128)(2,1)}, u32[]{:S(2)}, u32[]{:S(2)}) collective-permute-start(bf16[384,1536]{1,0:T(8,128)(2,1)} %get-tuple-element.77), channel_id=1, source_target_pairs={{0,8},{8,0},{16,24},{24,16},{1,9},{9,1},{17,25},{25,17},{2,10},{10... | collective-permute-start | bytes 3538952 | tf_op jit(solution)/shard_map/ppermute | solution.py:296
  135.7 39.1 %collective-permute-start.40 = (bf16[384,768]{1,0:T(8,128)(2,1)S(1)}, bf16[384,768]{1,0:T(8,128)(2,1)}, u32[]{:S(2)}, u32[]{:S(2)}) collective-permute-start(bf16[384,768]{1,0:T(8,128)(2,1)S(1)} %broadcast_select_fusion.2.c_ref), channel_id=1, source_target_pairs={{0,8},{8,0},{16,24},{24,16},{1,9},{9,1},{17,25},{25,17},{2,10},{10... | collective-permute-start | bytes 1769480 | tf_op jit(solution)/shard_map/ppermute | solution.py:296
  167.8 10.7 %collective-permute-start.9 = (bf16[384,1152]{1,0:T(8,128)(2,1)}, bf16[384,1152]{1,0:T(8,128)(2,1)}, u32[]{:S(2)}, u32[]{:S(2)}) collective-permute-start(bf16[384,1152]{1,0:T(8,128)(2,1)} %pad_maximum_fusion.2), channel_id=1, source_target_pairs={{0,8},{8,0},{16,24},{24,16},{1,9},{9,1},{17,25},{25,17},{2,10},{10... | collective-permute-start | bytes 2654216 | tf_op jit(solution)/shard_map/ppermute | solution.py:296
  171.2 19.2 %collective-permute-start.42 = (bf16[384,768]{1,0:T(8,128)(2,1)}, bf16[384,768]{1,0:T(8,128)(2,1)S(1)}, u32[]{:S(2)}, u32[]{:S(2)}) collective-permute-start(bf16[384,768]{1,0:T(8,128)(2,1)} %get-tuple-element.49), channel_id=1, source_target_pairs={{0,8},{8,0},{16,24},{24,16},{1,9},{9,1},{17,25},{25,17},{2,10},{10... | collective-permute-start | bytes 1769480 | tf_op jit(solution)/shard_map/ppermute | solution.py:296
  174.3 175.8 %collective-permute-start.5 = (bf16[384,768]{1,0:T(8,128)(2,1)S(1)}, bf16[384,768]{1,0:T(8,128)(2,1)S(1)}, u32[]{:S(2)}, u32[]{:S(2)}) collective-permute-start(bf16[384,768]{1,0:T(8,128)(2,1)S(1)} %copy-done.15), channel_id=1, source_target_pairs={{0,8},{8,0},{16,24},{24,16},{1,9},{9,1},{17,25},{25,17},{2,10},{10... | collective-permute-start | bytes 1769480 | tf_op jit(solution)/shard_map/ppermute | solution.py:296
  174.9 15.5 %collective-permute-start.43 = (bf16[384,1536]{1,0:T(8,128)(2,1)S(1)}, bf16[384,1536]{1,0:T(8,128)(2,1)S(1)}, u32[]{:S(2)}, u32[]{:S(2)}) collective-permute-start(bf16[384,1536]{1,0:T(8,128)(2,1)S(1)} %copy-done.14), channel_id=1, source_target_pairs={{0,8},{8,0},{16,24},{24,16},{1,9},{9,1},{17,25},{25,17},{2,10},{10... | collective-permute-start | bytes 3538952 | tf_op jit(solution)/shard_map/ppermute | solution.py:296
  196.1 14.5 %collective-permute-start.44 = (bf16[48,3072]{1,0:T(8,128)(2,1)S(1)}, bf16[48,3072]{1,0:T(8,128)(2,1)S(1)}, u32[]{:S(2)}, u32[]{:S(2)}) collective-permute-start(bf16[48,3072]{1,0:T(8,128)(2,1)S(1)} %constant_dynamic-slice_fusion), channel_id=1, source_target_pairs={{0,2},{2,4},{4,6},{6,7},{7,5},{5,3},{3,1},{1,0},{8,10},{10,12},{12... | collective-permute-start | bytes 884744 | tf_op jit(solution)/shard_map/ppermute | solution.py:339
  197.8 14.5 %collective-permute-start.58 = (bf16[48,3072]{1,0:T(8,128)(2,1)S(1)}, bf16[48,3072]{1,0:T(8,128)(2,1)S(1)}, u32[]{:S(2)}, u32[]{:S(2)}) collective-permute-start(bf16[48,3072]{1,0:T(8,128)(2,1)S(1)} %fusion.44), channel_id=1, source_target_pairs={{0,1},{2,0},{4,2},{6,4},{7,6},{5,7},{3,5},{1,3},{8,9},{10,8},{12,1... | collective-permute-start | bytes 884744 | tf_op jit(solution)/shard_map/ppermute | solution.py:339
  210.7 13.7 %collective-permute-start.45 = (bf16[48,3072]{1,0:T(8,128)(2,1)S(1)}, bf16[48,3072]{1,0:T(8,128)(2,1)S(1)}, u32[]{:S(2)}, u32[]{:S(2)}) collective-permute-start(bf16[48,3072]{1,0:T(8,128)(2,1)S(1)} %dynamic-slice_add_fusion.6), channel_id=1, source_target_pairs={{0,2},{2,4},{4,6},{6,7},{7,5},{5,3},{3,1},{1,0},{8,10},{10,12},{12... | collective-permute-start | bytes 884744 | tf_op jit(solution)/shard_map/ppermute | solution.py:339
  212.4 13.9 %collective-permute-start.59 = (bf16[48,3072]{1,0:T(8,128)(2,1)S(1)}, bf16[48,3072]{1,0:T(8,128)(2,1)S(1)}, u32[]{:S(2)}, u32[]{:S(2)}) collective-permute-start(bf16[48,3072]{1,0:T(8,128)(2,1)S(1)} %fusion.56), channel_id=1, source_target_pairs={{0,1},{2,0},{4,2},{6,4},{7,6},{5,7},{3,5},{1,3},{8,9},{10,8},{12,1... | collective-permute-start | bytes 884744 | tf_op jit(solution)/shard_map/ppermute | solution.py:339
  224.4 10.9 %collective-permute-start.46 = (bf16[48,3072]{1,0:T(8,128)(2,1)S(1)}, bf16[48,3072]{1,0:T(8,128)(2,1)S(1)}, u32[]{:S(2)}, u32[]{:S(2)}) collective-permute-start(bf16[48,3072]{1,0:T(8,128)(2,1)S(1)} %dynamic-slice_add_fusion.5), channel_id=1, source_target_pairs={{0,2},{2,4},{4,6},{6,7},{7,5},{5,3},{3,1},{1,0},{8,10},{10,12},{12... | collective-permute-start | bytes 884744 | tf_op jit(solution)/shard_map/ppermute | solution.py:339
  226.4 10.7 %collective-permute-start.60 = (bf16[48,3072]{1,0:T(8,128)(2,1)S(1)}, bf16[48,3072]{1,0:T(8,128)(2,1)S(1)}, u32[]{:S(2)}, u32[]{:S(2)}) collective-permute-start(bf16[48,3072]{1,0:T(8,128)(2,1)S(1)} %fusion.55), channel_id=1, source_target_pairs={{0,1},{2,0},{4,2},{6,4},{7,6},{5,7},{3,5},{1,3},{8,9},{10,8},{12,1... | collective-permute-start | bytes 884744 | tf_op jit(solution)/shard_map/ppermute | solution.py:339
  229.1 9.3 %collective-permute-start.19 = (bf16[48,1536]{1,0:T(8,128)(2,1)S(1)}, bf16[48,1536]{1,0:T(8,128)(2,1)S(1)}, u32[]{:S(2)}, u32[]{:S(2)}) collective-permute-start(bf16[48,1536]{1,0:T(8,128)(2,1)S(1)} %get-tuple-element.68), channel_id=1, source_target_pairs={{0,2},{2,4},{4,6},{6,7},{7,5},{5,3},{3,1},{1,0},{8,10},{10,12},{12... | collective-permute-start | bytes 442376 | tf_op jit(solution)/shard_map/ppermute | solution.py:339
  230.9 9.3 %collective-permute-start.33 = (bf16[48,1536]{1,0:T(8,128)(2,1)S(1)}, bf16[48,1536]{1,0:T(8,128)(2,1)S(1)}, u32[]{:S(2)}, u32[]{:S(2)}) collective-permute-start(bf16[48,1536]{1,0:T(8,128)(2,1)S(1)} %get-tuple-element.66), channel_id=1, source_target_pairs={{0,1},{2,0},{4,2},{6,4},{7,6},{5,7},{3,5},{1,3},{8,9},{10,8},{12,1... | collective-permute-start | bytes 442376 | tf_op jit(solution)/shard_map/ppermute | solution.py:339
  235.4 12.5 %collective-permute-start.47 = (bf16[48,3072]{1,0:T(8,128)(2,1)S(1)}, bf16[48,3072]{1,0:T(8,128)(2,1)S(1)}, u32[]{:S(2)}, u32[]{:S(2)}) collective-permute-start(bf16[48,3072]{1,0:T(8,128)(2,1)S(1)} %dynamic-slice_add_fusion.4), channel_id=1, source_target_pairs={{0,2},{2,4},{4,6},{6,7},{7,5},{5,3},{3,1},{1,0},{8,10},{10,12},{12... | collective-permute-start | bytes 884744 | tf_op jit(solution)/shard_map/ppermute | solution.py:339
  237.1 12.5 %collective-permute-start.61 = (bf16[48,3072]{1,0:T(8,128)(2,1)S(1)}, bf16[48,3072]{1,0:T(8,128)(2,1)S(1)}, u32[]{:S(2)}, u32[]{:S(2)}) collective-permute-start(bf16[48,3072]{1,0:T(8,128)(2,1)S(1)} %fusion.54), channel_id=1, source_target_pairs={{0,1},{2,0},{4,2},{6,4},{7,6},{5,7},{3,5},{1,3},{8,9},{10,8},{12,1... | collective-permute-start | bytes 884744 | tf_op jit(solution)/shard_map/ppermute | solution.py:339
  248.0 13.4 %collective-permute-start.48 = (bf16[48,3072]{1,0:T(8,128)(2,1)S(1)}, bf16[48,3072]{1,0:T(8,128)(2,1)S(1)}, u32[]{:S(2)}, u32[]{:S(2)}) collective-permute-start(bf16[48,3072]{1,0:T(8,128)(2,1)S(1)} %dynamic-slice_add_fusion.3), channel_id=1, source_target_pairs={{0,2},{2,4},{4,6},{6,7},{7,5},{5,3},{3,1},{1,0},{8,10},{10,12},{12... | collective-permute-start | bytes 884744 | tf_op jit(solution)/shard_map/ppermute | solution.py:339
  249.7 13.4 %collective-permute-start.62 = (bf16[48,3072]{1,0:T(8,128)(2,1)S(1)}, bf16[48,3072]{1,0:T(8,128)(2,1)S(1)}, u32[]{:S(2)}, u32[]{:S(2)}) collective-permute-start(bf16[48,3072]{1,0:T(8,128)(2,1)S(1)} %fusion.53), channel_id=1, source_target_pairs={{0,1},{2,0},{4,2},{6,4},{7,6},{5,7},{3,5},{1,3},{8,9},{10,8},{12,1... | collective-permute-start | bytes 884744 | tf_op jit(solution)/shard_map/ppermute | solution.py:339
  261.5 13.4 %collective-permute-start.49 = (bf16[48,3072]{1,0:T(8,128)(2,1)S(1)}, bf16[48,3072]{1,0:T(8,128)(2,1)S(1)}, u32[]{:S(2)}, u32[]{:S(2)}) collective-permute-start(bf16[48,3072]{1,0:T(8,128)(2,1)S(1)} %dynamic-slice_add_fusion.2), channel_id=1, source_target_pairs={{0,2},{2,4},{4,6},{6,7},{7,5},{5,3},{3,1},{1,0},{8,10},{10,12},{12... | collective-permute-start | bytes 884744 | tf_op jit(solution)/shard_map/ppermute | solution.py:339
  263.2 13.4 %collective-permute-start.63 = (bf16[48,3072]{1,0:T(8,128)(2,1)S(1)}, bf16[48,3072]{1,0:T(8,128)(2,1)S(1)}, u32[]{:S(2)}, u32[]{:S(2)}) collective-permute-start(bf16[48,3072]{1,0:T(8,128)(2,1)S(1)} %fusion.52), channel_id=1, source_target_pairs={{0,1},{2,0},{4,2},{6,4},{7,6},{5,7},{3,5},{1,3},{8,9},{10,8},{12,1... | collective-permute-start | bytes 884744 | tf_op jit(solution)/shard_map/ppermute | solution.py:339
  275.0 9.2 %collective-permute-start.50 = (bf16[48,3072]{1,0:T(8,128)(2,1)S(1)}, bf16[48,3072]{1,0:T(8,128)(2,1)S(1)}, u32[]{:S(2)}, u32[]{:S(2)}) collective-permute-start(bf16[48,3072]{1,0:T(8,128)(2,1)S(1)} %dynamic-slice_add_fusion.1), channel_id=1, source_target_pairs={{0,2},{2,4},{4,6},{6,7},{7,5},{5,3},{3,1},{1,0},{8,10},{10,12},{12... | collective-permute-start | bytes 884744 | tf_op jit(solution)/shard_map/ppermute | solution.py:339
  276.7 9.5 %collective-permute-start.64 = (bf16[48,3072]{1,0:T(8,128)(2,1)S(1)}, bf16[48,3072]{1,0:T(8,128)(2,1)S(1)}, u32[]{:S(2)}, u32[]{:S(2)}) collective-permute-start(bf16[48,3072]{1,0:T(8,128)(2,1)S(1)} %fusion.51), channel_id=1, source_target_pairs={{0,1},{2,0},{4,2},{6,4},{7,6},{5,7},{3,5},{1,3},{8,9},{10,8},{12,1... | collective-permute-start | bytes 884744 | tf_op jit(solution)/shard_map/ppermute | solution.py:339
  316.9 9.8 %collective-permute-start.55 = (bf16[48,3072]{1,0:T(8,128)(2,1)S(1)}, bf16[48,3072]{1,0:T(8,128)(2,1)S(1)}, u32[]{:S(2)}, u32[]{:S(2)}) collective-permute-start(bf16[48,3072]{1,0:T(8,128)(2,1)S(1)} %collective-permute-done.54), channel_id=1, source_target_pairs={{0,2},{2,4},{4,6},{6,7},{7,5},{5,3},{3,1},{1,0},{8,10},{10,12},{12... | collective-permute-start | bytes 884744 | tf_op jit(solution)/shard_map/ppermute | solution.py:339
  318.5 9.8 %collective-permute-start.69 = (bf16[48,3072]{1,0:T(8,128)(2,1)S(1)}, bf16[48,3072]{1,0:T(8,128)(2,1)S(1)}, u32[]{:S(2)}, u32[]{:S(2)}) collective-permute-start(bf16[48,3072]{1,0:T(8,128)(2,1)S(1)} %collective-permute-done.68), channel_id=1, source_target_pairs={{0,1},{2,0},{4,2},{6,4},{7,6},{5,7},{3,5},{1,3},{8,9},{10,8},{12,1... | collective-permute-start | bytes 884744 | tf_op jit(solution)/shard_map/ppermute | solution.py:339
  348.6 45.0 %collective-permute-start.72 = (bf16[768,1536]{1,0:T(8,128)(2,1)}, bf16[768,1536]{1,0:T(8,128)(2,1)}, u32[]{:S(2)}, u32[]{:S(2)}) collective-permute-start(bf16[768,1536]{1,0:T(8,128)(2,1)} %get-tuple-element.63), channel_id=1, source_target_pairs={{0,8},{8,0},{16,24},{24,16},{1,9},{9,1},{17,25},{25,17},{2,10},{10... | collective-permute-start | bytes 7077896 | tf_op jit(solution)/shard_map/ppermute | solution.py:296
  350.1 40.6 %collective-permute-start.7 = (bf16[384,768]{1,0:T(8,128)(2,1)}, bf16[384,768]{1,0:T(8,128)(2,1)}, u32[]{:S(2)}, u32[]{:S(2)}) collective-permute-start(bf16[384,768]{1,0:T(8,128)(2,1)} %broadcast_select_fusion), channel_id=1, source_target_pairs={{0,8},{8,0},{16,24},{24,16},{1,9},{9,1},{17,25},{25,17},{2,10},{10... | collective-permute-start | bytes 1769480 | tf_op jit(solution)/shard_map/ppermute | solution.py:296
  (77 other events, 432.2 us)
